TPU v7x, 768 devices: a whole 4x8x12 slice. The times are simulated.
768 devices in a mesh: region: 768 (over x, z, y, core).
Axes of the slice: x: 4, y: 8, z: 12, core: 2. Of those that a mesh axis runs over, the one named last changes fastest.
Arguments:
- right_side: float32 [393216, 512], P('region'), may hold values from -6 to 6
- smoother: float32 [3072, 128, 128], P('region')
- diagonal_blocks: float32 [3072, 128, 128], P('region')
- couplings: float32 [3072, 128, 128], P('region'), may hold values from -0.5 to 0.5
- grad_blocks: float32 [3072, 2, 128, 128], P('region'), may hold values from -0.5 to 0.5
- grad_pattern: int32 [3072, 2], P('region'), may hold values from 0 to 1
- interp_blocks: float32 [3072, 2, 128, 128], P('region'), may hold values from -0.5 to 0.5
- interp_pattern: int32 [3072, 2], P('region'), may hold values from 0 to 3
- node_smoother: float32 [768, 128, 128], P('region')
- vector_smoother: float32 [2304, 128, 128], P('region')
- node_aggregates: int32 [98304], P('region'), may hold values from 0 to 15
- vector_aggregates: int32 [294912], P('region'), may hold values from 0 to 47
- node_coarse: float32 [98304, 128], P('region')
- vector_coarse: float32 [98304, 128], P('region')
Outputs:
- correction: float32 [393216, 512], P('region')
Inputs may be any that keep to these rules, and one draw needn't show every extreme that they name: `grad_pattern`: value 1 names the first node block of the next region. `interp_pattern`: value 3 names the first vector-nodal block of the next region.
All inputs are finite; a program needn't handle non-finite values.
Results may differ from a plain program's by a relative error of at most 0.0003.
Values sent between devices are 32-bit elements; how exact they have to be, the bound alone decides.
No kernel may reach another device: no remote copies, remote signals or barrier semaphores. Data moves between devices by JAX's collectives and lax.ppermute only.
A program may use at most 32 MiB of HBM per device.

v0:
```python
import jax
import jax.numpy as jnp
from jax import lax
from jax.sharding import PartitionSpec as P


def passed_along(x, axis, by):
    size = lax.axis_size(axis)
    pairs = [(i, i + by) for i in range(size) if 0 <= i + by < size]
    return lax.ppermute(x, axis, pairs)


def multiply(formula, left, right):
    return jnp.einsum(
        formula, left, right, precision=lax.Precision.HIGHEST, preferred_element_type=jnp.float32
    )


def restrict_blocks(blocks, pattern, resid, amount):
    onehot = (pattern[:, :, None] == jnp.arange(amount + 1, dtype=jnp.int32)[None, None, :]).astype(
        jnp.float32
    )
    products_all = multiply("ksij,kir->ksjr", blocks, resid)
    return multiply("ksc,ksjr->cjr", onehot, products_all)


def prolong_blocks(blocks, pattern, extended, amount):
    onehot = (pattern[:, :, None] == jnp.arange(amount + 1, dtype=jnp.int32)[None, None, :]).astype(
        jnp.float32
    )
    picked = multiply("ksc,cjr->ksjr", onehot, extended)
    return multiply("ksij,ksjr->kir", blocks, picked)


def auxiliary_solve(aux_resid, block_smoother, aggregates, coarse_op):
    amount, width, vectors = aux_resid.shape
    fixed = multiply("cij,cjr->cir", block_smoother, aux_resid)
    onehot = (aggregates[:, None] == jnp.arange(width, dtype=jnp.int32)[None, :]).astype(
        jnp.float32
    )
    flattened = aux_resid.reshape(amount * width, vectors)
    coarse = multiply("nc,nr->cr", onehot, flattened)
    coarse_fix = multiply("ij,jr->ir", coarse_op, coarse)
    return fixed + multiply("nc,cr->nr", onehot, coarse_fix).reshape(amount, width, vectors)


def local(
    right_side,
    smoother,
    diagonal_blocks,
    couplings,
    grad_blocks,
    grad_pattern,
    interp_blocks,
    interp_pattern,
    node_smoother,
    vector_smoother,
    node_aggregates,
    vector_aggregates,
    node_coarse,
    vector_coarse,
):
    blocks_here, width, _ = smoother.shape
    vectors = right_side.shape[1]
    node_count = node_smoother.shape[0]
    vector_count = vector_smoother.shape[0]
    source = right_side.reshape(blocks_here, width, vectors)
    smoothed = multiply("kij,kjr->kir", smoother, source)
    next_first = passed_along(smoothed[0], "region", -1)
    outgoing = multiply("ji,jr->ir", couplings[-1], smoothed[-1])
    before_term = passed_along(outgoing, "region", 1)
    following = jnp.concatenate([smoothed[1:], next_first[None]], axis=0)
    forward = multiply("kij,kjr->kir", couplings, following)
    backward = jnp.concatenate(
        [before_term[None], multiply("kji,kjr->kir", couplings[:-1], smoothed[:-1])], axis=0
    )
    resid = source - (multiply("kij,kjr->kir", diagonal_blocks, smoothed) + forward + backward)
    node_ext = restrict_blocks(grad_blocks, grad_pattern, resid, node_count)
    vector_ext = restrict_blocks(interp_blocks, interp_pattern, resid, vector_count)
    incoming = passed_along((node_ext[node_count], vector_ext[vector_count]), "region", 1)
    node_resid = node_ext[:node_count].at[0].add(incoming[0])
    vector_resid = vector_ext[:vector_count].at[0].add(incoming[1])
    node_fix = auxiliary_solve(node_resid, node_smoother, node_aggregates, node_coarse)
    vector_fix = auxiliary_solve(vector_resid, vector_smoother, vector_aggregates, vector_coarse)
    returned = passed_along((node_fix[0], vector_fix[0]), "region", -1)
    node_extended = jnp.concatenate([node_fix, returned[0][None]], axis=0)
    vector_extended = jnp.concatenate([vector_fix, returned[1][None]], axis=0)
    added = prolong_blocks(grad_blocks, grad_pattern, node_extended, node_count) + prolong_blocks(
        interp_blocks, interp_pattern, vector_extended, vector_count
    )
    return (smoothed + added).reshape(blocks_here * width, vectors)


def solution(mesh):
    in_specs = (
        P("region", None),
        P("region", None, None),
        P("region", None, None),
        P("region", None, None),
        P("region", None, None, None),
        P("region", None),
        P("region", None, None, None),
        P("region", None),
        P("region", None, None),
        P("region", None, None),
        P("region"),
        P("region"),
        P("region", None),
        P("region", None),
    )
    out_specs = P("region", None)
    return jax.shard_map(local, mesh=mesh, in_specs=in_specs, out_specs=out_specs, check_vma=False)
```

profile of v0, /device:TPU:6, one launch (start us, length us, event | category | flops | bytes accessed | tf_op | source)
XLA Modules:
  0.0 102.5 jit_solution(11749857317606984100)
XLA Ops:
  0.0 2.4 %fusion.68 = f32[4,128,512]{2,1,0:T(8,128)S(1)} fusion(f32[4,128,128]{2,1,0:T(8,128)} %param.19, f32[4,128,512]{2,1,0:T(8,128)} %bitcast.138), kind=kOutput, calls=%fused_computation.68 | convolution fusion | flops 402653184 | bytes 2359296 | tf_op jit(solution)/shard_map/kij,kjr->kir/dot_general | solution.py:14
  2.5 0.0 copy-start.7
  2.5 17.3 %collective-permute-start = (f32[128,512]{1,0:T(8,128)S(1)}, f32[128,512]{1,0:T(8,128)}, u32[]{:S(2)}, u32[]{:S(2)}) collective-permute-start(f32[128,512]{1,0:T(8,128)S(1)} %slice_bitcast_fusion.3), channel_id=1, source_target_pairs={{1,0},{2,1},{3,2},{4,3},{5,4},{6,5},{7,6},{8,7},{9,8},{10,9},{11,1... | collective-permute-start | bytes 786440 | tf_op jit(solution)/shard_map/ppermute | solution.py:10
  19.8 1.3 %convolution_bitcast_fusion.3 = f32[128,512]{0,1:T(8,128)} fusion(f32[4,128,512]{2,1,0:T(8,128)S(1)} %fusion.68, f32[4,128,128]{2,1,0:T(8,128)S(1)} %copy-done.6), kind=kOutput, calls=%fused_computation.25 | convolution fusion | flops 100663296 | bytes 589824 | tf_op jit(solution)/shard_map/ji,jr->ir/dot_general | solution.py:14
  21.1 1.9 %collective-permute-start.1 = (f32[128,512]{0,1:T(8,128)}, f32[128,512]{0,1:T(8,128)}, u32[]{:S(2)}, u32[]{:S(2)}) collective-permute-start(f32[128,512]{0,1:T(8,128)} %convolution_bitcast_fusion.3), channel_id=1, source_target_pairs={{0,1},{1,2},{2,3},{3,4},{4,5},{5,6},{6,7},{7,8},{8,9},{9,10},{10,1... | collective-permute-start | bytes 786440 | tf_op jit(solution)/shard_map/ppermute | solution.py:10
  23.1 1.3 %copy.27 = f32[4,128,512]{1,2,0:T(8,128)} copy(f32[4,128,512]{2,1,0:T(8,128)S(1)} %bitcast.139) | data formatting | bytes 2097152 | tf_op jit(solution)/shard_map/reshape | solution.py:67
  24.4 0.1 slice.87
  24.4 0.0 copy-start.2
  24.4 1.8 %fusion.69 = f32[4,512,128]{2,1,0:T(8,128)S(1)} fusion(f32[4,128,512]{2,1,0:T(8,128)S(1)} %fusion.68, f32[4,128,128]{2,1,0:T(8,128)S(1)} %copy-done.7), kind=kOutput, calls=%fused_computation.69 | convolution fusion | flops 402653184 | bytes 2359296 | tf_op jit(solution)/shard_map/kij,kjr->kir/dot_general | solution.py:14
  26.2 1.4 %convolution_bitcast_fusion = f32[3,128,512]{1,2,0:T(8,128)S(1)} fusion(f32[4,128,512]{2,1,0:T(8,128)S(1)} %fusion.68, f32[4,128,128]{2,1,0:T(8,128)S(1)} %copy-done.6), kind=kOutput, calls=%fused_computation.19 | convolution fusion | flops 301989888 | bytes 2031616 | tf_op jit(solution)/shard_map/kji,kjr->kir/dot_general | solution.py:14
  27.7 5.7 %collective-permute-done.1 = f32[128,512]{0,1:T(8,128)} collective-permute-done((f32[128,512]{0,1:T(8,128)}, f32[128,512]{0,1:T(8,128)}, u32[]{:S(2)}, u32[]{:S(2)}) %collective-permute-start.1) | collective-permute-done | bytes 262176 | tf_op jit(solution)/shard_map/ppermute | solution.py:10
  33.3 2.9 %fusion.20 = f32[4,128,512,1]{1,2,3,0:T(8,128)S(1)} fusion(f32[4,128,512]{1,2,0:T(8,128)S(1)} %copy-done.2, f32[4,512,128]{2,1,0:T(8,128)S(1)} %fusion.69, f32[4,128,128]{2,1,0:T(8,128)S(1)} %copy-done.6, f32[1,128,512]{2,1,0:T(8,128)} %bitcast.4, f32[3,128,512]{2,1,0:T(8,128)S(1)} %slice.87, f32[3,128,512]{1,2,0:T(8,128)S(1)} %convolution_bitcast_fusion, ...), kind=kOutput, calls=%fused_computation.15 | convolution fusion | flops 403963904 | bytes 5505024 | tf_op jit(solution)/shard_map/kij,kjr->kir/dot_general | solution.py:14
  36.3 3.1 %fusion.70 = f32[4,512,2,128]{3,1,2,0:T(8,128)} fusion(f32[4,128,512,1]{1,2,3,0:T(8,128)S(1)} %fusion.20, f32[4,2,128,128]{3,2,1,0:T(8,128)S(1)} %copy-done), kind=kOutput, calls=%fused_computation.70 | convolution fusion | flops 805306368 | bytes 3670016 | tf_op jit(solution)/shard_map/ksij,kir->ksjr/dot_general | solution.py:14
  39.4 3.1 %copy.39 = f32[4,512,2,128]{1,0,2,3:T(4,128)} copy(f32[4,512,2,128]{3,1,2,0:T(8,128)} %fusion.70) | data formatting | bytes 4194304 | tf_op jit(solution)/shard_map/ksij,kir->ksjr/dot_general | solution.py:14
  42.5 3.4 %fusion.31 = f32[2,128,512]{2,0,1:T(2,128)S(1)} fusion(f32[4,512,2,128]{1,0,2,3:T(4,128)} %copy.39, s32[4,2]{0,1:T(2,128)S(1)} %copy-done.11), kind=kOutput, calls=%fused_computation.22 | convolution fusion | flops 12582928 | bytes 2621472 | tf_op jit(solution)/shard_map/ksc,ksjr->cjr/dot_general | solution.py:14
  45.9 1.1 %fusion.67 = (f32[1,128,512]{2,0,1:T(1,128)S(1)}, f32[1,128,512]{2,0,1:T(1,128)}) fusion(f32[2,128,512]{2,0,1:T(2,128)S(1)} %fusion.31), kind=kLoop, calls=%fused_computation.67 | loop fusion | bytes 1048576 | tf_op jit(solution)/shard_map/slice | solution.py:80
  47.0 0.7 copy.79
  47.8 2.1 %collective-permute-start.2 = (f32[128,512]{1,0:T(8,128)}, f32[128,512]{1,0:T(8,128)}, u32[]{:S(2)}, u32[]{:S(2)}) collective-permute-start(f32[128,512]{1,0:T(8,128)} %bitcast.134), channel_id=1, source_target_pairs={{0,1},{1,2},{2,3},{3,4},{4,5},{5,6},{6,7},{7,8},{8,9},{9,10},{10,1... | collective-permute-start | bytes 786440 | tf_op jit(solution)/shard_map/ppermute | solution.py:10
  49.9 3.1 %fusion.72 = f32[4,512,2,128]{3,1,2,0:T(8,128)} fusion(f32[4,128,512,1]{1,2,3,0:T(8,128)S(1)} %fusion.20, f32[4,2,128,128]{3,2,1,0:T(8,128)S(1)} %copy-done.3), kind=kOutput, calls=%fused_computation.72 | convolution fusion | flops 805306368 | bytes 3670016 | tf_op jit(solution)/shard_map/ksij,kir->ksjr/dot_general | solution.py:14
  53.0 3.1 %copy.46 = f32[4,512,2,128]{1,0,2,3:T(4,128)} copy(f32[4,512,2,128]{3,1,2,0:T(8,128)} %fusion.72) | data formatting | bytes 4194304 | tf_op jit(solution)/shard_map/ksij,kir->ksjr/dot_general | solution.py:14
  56.1 0.0 copy-start.8
  56.1 3.4 %fusion.14 = f32[4,128,512]{2,0,1:T(4,128)S(1)} fusion(f32[4,512,2,128]{1,0,2,3:T(4,128)} %copy.46, s32[4,2]{0,1:T(2,128)S(1)} %copy-done.12), kind=kOutput, calls=%fused_computation.10 | convolution fusion | flops 25165856 | bytes 3145760 | tf_op jit(solution)/shard_map/ksc,ksjr->cjr/dot_general | solution.py:14
  59.5 0.4 fusion.66
  60.0 1.9 %collective-permute-start.4 = (f32[128,512]{1,0:T(8,128)S(1)}, f32[128,512]{1,0:T(8,128)S(1)}, u32[]{:S(2)}, u32[]{:S(2)}) collective-permute-start(f32[128,512]{1,0:T(8,128)S(1)} %bitcast.141), channel_id=1, source_target_pairs={{0,1},{1,2},{2,3},{3,4},{4,5},{5,6},{6,7},{7,8},{8,9},{9,10},{10,1... | collective-permute-start | bytes 786440 | tf_op jit(solution)/shard_map/ppermute | solution.py:10
  61.9 1.3 %fusion.42 = f32[128,512]{1,0:T(8,128)S(1)} fusion(f32[1,128,512]{2,0,1:T(1,128)S(1)} %copy-done.5, f32[128,512]{1,0:T(8,128)} %collective-permute-done.2, s32[128]{0:T(128)S(1)} %copy-done.14), kind=kOutput, calls=%fused_computation.43 | convolution fusion | flops 100745216 | bytes 786944 | tf_op jit(solution)/shard_map/nc,nr->cr/dot_general | solution.py:14
  63.3 0.6 fusion.71
  63.9 0.4 fusion.49
  64.3 2.2 %fusion.34 = f32[128,512]{0,1:T(8,128)} fusion(f32[128,512]{0,1:T(8,128)S(1)} %fusion.49, f32[1,128,512]{2,0,1:T(1,128)S(1)} %copy-done.5, f32[128,512]{1,0:T(8,128)} %collective-permute-done.2, f32[1,128,128]{2,1,0:T(8,128)S(1)} %copy-done.9), kind=kOutput, calls=%fused_computation.24 | convolution fusion | flops 100794368 | bytes 1114112 | tf_op jit(solution)/shard_map/cij,cjr->cir/dot_general | solution.py:14
  66.5 8.0 %collective-permute-start.3 = (f32[128,512]{0,1:T(8,128)}, f32[128,512]{0,1:T(8,128)}, u32[]{:S(2)}, u32[]{:S(2)}) collective-permute-start(f32[128,512]{0,1:T(8,128)} %fusion.34), channel_id=1, source_target_pairs={{1,0},{2,1},{3,2},{4,3},{5,4},{6,5},{7,6},{8,7},{9,8},{10,9},{11,1... | collective-permute-start | bytes 786440 | tf_op jit(solution)/shard_map/ppermute | solution.py:10
  74.5 0.0 copy-start.10
  74.6 0.3 copy.31
  74.8 2.5 %scatter-add.4 = f32[3,128,512]{2,0,1:T(4,128)S(1)} dynamic-update-slice(f32[3,128,512]{2,0,1:T(4,128)S(1)} %bitcast.137, f32[1,128,512]{2,0,1:T(1,128)S(1)} %copy.31, s32[]{:T(128)} %constant.47.clone.1, s32[]{:T(128)} %constant.47.clone.1, s32[]{:T(128)} %constant.47.clone.1) | dynamic-update-slice | bytes 524292 | tf_op jit(solution)/shard_map/scatter-add | solution.py:82
  77.3 0.3 copy.33
  77.6 0.5 fusion.40
  78.1 0.6 fusion.73
  78.7 0.5 fusion.39
  79.2 1.1 %copy.34 = f32[3,128,512]{1,2,0:T(8,128)} copy(f32[3,128,512]{2,1,0:T(8,128)S(1)} %bitcast.140) | data formatting | bytes 1572864 | tf_op jit(solution)/shard_map/reshape | solution.py:44
  80.4 2.6 %fusion.30 = f32[3,128,512]{1,2,0:T(8,128)S(1)} fusion(f32[3,128,512]{1,2,0:T(8,128)} %copy.34, f32[3,128,512]{2,1,0:T(8,128)S(1)} %copy.33, f32[3,128,128]{2,1,0:T(8,128)} %param.27), kind=kOutput, calls=%fused_computation.21 | convolution fusion | flops 302186496 | bytes 2555904 | tf_op jit(solution)/shard_map/cij,cjr->cir/dot_general | solution.py:14
  83.0 0.7 slice_bitcast_fusion
  83.7 2.6 %collective-permute-start.5 = (f32[128,512]{0,1:T(8,128)}, f32[128,512]{0,1:T(8,128)}, u32[]{:S(2)}, u32[]{:S(2)}) collective-permute-start(f32[128,512]{0,1:T(8,128)} %slice_bitcast_fusion), channel_id=1, source_target_pairs={{1,0},{2,1},{3,2},{4,3},{5,4},{6,5},{7,6},{8,7},{9,8},{10,9},{11,1... | collective-permute-start | bytes 786440 | tf_op jit(solution)/shard_map/ppermute | solution.py:10
  86.4 1.1 %maximum_bitcast_fusion.1 = f32[2,128,512,1]{1,2,0,3:T(8,128)S(1)} fusion(f32[1,128,512]{1,2,0:T(8,128)} %bitcast.21, f32[1,128,512]{1,2,0:T(8,128)} %bitcast.20), kind=kLoop, calls=%fused_computation.30 | loop fusion | flops 131072 | bytes 1048576 | tf_op jit(solution)/shard_map/concatenate | solution.py:86
  87.4 0.2 copy.43
  87.7 2.1 %fusion.58 = f32[4,2,128,512]{3,0,2,1:T(4,128)S(1)} fusion(f32[2,128,512,1]{2,0,1,3:T(2,128)S(1)} %copy.43, s32[4,2]{0,1:T(2,128)S(1)} %copy-done.11), kind=kOutput, calls=%fused_computation.57 | convolution fusion | flops 12582928 | bytes 2621472 | tf_op jit(solution)/shard_map/ksc,cjr->ksjr/dot_general | solution.py:14
  89.8 1.9 %fusion.8 = f32[4,512,128]{1,2,0:T(8,128)S(1)} fusion(f32[4,2,128,128]{3,2,1,0:T(8,128)S(1)} %copy-done, f32[4,2,128,512]{3,0,2,1:T(4,128)S(1)} %fusion.58), kind=kOutput, calls=%fused_computation.8 | convolution fusion | flops 805306368 | bytes 3670016 | tf_op jit(solution)/shard_map/ksij,ksjr->kir/dot_general | solution.py:14
  91.7 2.0 %maximum_bitcast_fusion = f32[4,128,512,1]{1,2,0,3:T(8,128)} fusion(f32[1,128,512]{1,2,0:T(8,128)} %bitcast.36, f32[3,128,512]{1,2,0:T(8,128)S(1)} %fusion.30), kind=kLoop, calls=%fused_computation.29 | loop fusion | flops 262144 | bytes 2097152 | tf_op jit(solution)/shard_map/concatenate | solution.py:87
  93.7 2.6 %copy.49 = f32[4,128,512,1]{2,0,1,3:T(4,128)} copy(f32[4,128,512,1]{1,2,0,3:T(8,128)} %maximum_bitcast_fusion) | data formatting | bytes 2097152 | tf_op jit(solution)/shard_map/concatenate | solution.py:87
  96.3 3.2 %fusion.56 = f32[4,2,128,512]{3,0,2,1:T(4,128)S(1)} fusion(f32[4,128,512,1]{2,0,1,3:T(4,128)} %copy.49, s32[4,2]{0,1:T(2,128)S(1)} %copy-done.12), kind=kOutput, calls=%fused_computation.56 | convolution fusion | flops 25165856 | bytes 3145760 | tf_op jit(solution)/shard_map/ksc,cjr->ksjr/dot_general | solution.py:14
  99.6 2.9 %fusion.27 = f32[4,128,512]{2,1,0:T(8,128)} fusion(f32[4,128,512]{2,1,0:T(8,128)S(1)} %fusion.68, f32[4,512,128]{1,2,0:T(8,128)S(1)} %fusion.8, f32[4,2,128,128]{3,2,1,0:T(8,128)S(1)} %copy-done.4, f32[4,2,128,512]{3,0,2,1:T(4,128)S(1)} %fusion.56), kind=kOutput, calls=%fused_computation.18 | convolution fusion | flops 805830656 | bytes 5767168 | tf_op jit(solution)/shard_map/ksij,ksjr->kir/dot_general | solution.py:14
  (34 shorter events, 0.1 us)
Async XLA Ops:
  0.0 36.2 %copy-start = (f32[4,2,128,128]{3,2,1,0:T(8,128)S(1)}, f32[4,2,128,128]{3,2,1,0:T(8,128)}, u32[]{:S(2)}) copy-start(f32[4,2,128,128]{3,2,1,0:T(8,128)} %param.22) | copy-start | bytes 1572868
  0.0 23.0 %copy-start.1 = (f32[512,512]{1,0:T(8,128)S(1)}, f32[512,512]{1,0:T(8,128)}, u32[]{:S(2)}) copy-start(f32[512,512]{1,0:T(8,128)} %param.18) | copy-start | bytes 3145732
  0.0 19.8 %copy-start.6 = (f32[4,128,128]{2,1,0:T(8,128)S(1)}, f32[4,128,128]{2,1,0:T(8,128)}, u32[]{:S(2)}) copy-start(f32[4,128,128]{2,1,0:T(8,128)} %param.21) | copy-start | bytes 786436
  2.5 21.9 %copy-start.7 = (f32[4,128,128]{2,1,0:T(8,128)S(1)}, f32[4,128,128]{2,1,0:T(8,128)}, u32[]{:S(2)}) copy-start(f32[4,128,128]{2,1,0:T(8,128)} %param.20) | copy-start | bytes 786436
  2.5 25.2 %collective-permute-start = (f32[128,512]{1,0:T(8,128)S(1)}, f32[128,512]{1,0:T(8,128)}, u32[]{:S(2)}, u32[]{:S(2)}) collective-permute-start(f32[128,512]{1,0:T(8,128)S(1)} %slice_bitcast_fusion.3), channel_id=1, source_target_pairs={{1,0},{2,1},{3,2},{4,3},{5,4},{6,5},{7,6},{8,7},{9,8},{10,9},{11,1... | collective-permute-start | bytes 786440 | tf_op jit(solution)/shard_map/ppermute | solution.py:10
  21.1 12.2 %collective-permute-start.1 = (f32[128,512]{0,1:T(8,128)}, f32[128,512]{0,1:T(8,128)}, u32[]{:S(2)}, u32[]{:S(2)}) collective-permute-start(f32[128,512]{0,1:T(8,128)} %convolution_bitcast_fusion.3), channel_id=1, source_target_pairs={{0,1},{1,2},{2,3},{3,4},{4,5},{5,6},{6,7},{7,8},{8,9},{9,10},{10,1... | collective-permute-start | bytes 786440 | tf_op jit(solution)/shard_map/ppermute | solution.py:10
  24.4 8.9 %copy-start.2 = (f32[4,128,512]{1,2,0:T(8,128)S(1)}, f32[4,128,512]{1,2,0:T(8,128)}, u32[]{:S(2)}) copy-start(f32[4,128,512]{1,2,0:T(8,128)} %copy.27) | copy-start | bytes 3145732
  39.4 3.1 %copy-start.11 = (s32[4,2]{0,1:T(2,128)S(1)}, s32[4,2]{0,1:T(2,128)}, u32[]{:S(2)}) copy-start(s32[4,2]{0,1:T(2,128)} %param.23) | copy-start | bytes 100
  42.5 7.4 %copy-start.3 = (f32[4,2,128,128]{3,2,1,0:T(8,128)S(1)}, f32[4,2,128,128]{3,2,1,0:T(8,128)}, u32[]{:S(2)}) copy-start(f32[4,2,128,128]{3,2,1,0:T(8,128)} %param.24) | copy-start | bytes 1572868
  47.8 14.1 %collective-permute-start.2 = (f32[128,512]{1,0:T(8,128)}, f32[128,512]{1,0:T(8,128)}, u32[]{:S(2)}, u32[]{:S(2)}) collective-permute-start(f32[128,512]{1,0:T(8,128)} %bitcast.134), channel_id=1, source_target_pairs={{0,1},{1,2},{2,3},{3,4},{4,5},{5,6},{6,7},{7,8},{8,9},{9,10},{10,1... | collective-permute-start | bytes 786440 | tf_op jit(solution)/shard_map/ppermute | solution.py:10
  53.0 3.1 %copy-start.12 = (s32[4,2]{0,1:T(2,128)S(1)}, s32[4,2]{0,1:T(2,128)}, u32[]{:S(2)}) copy-start(s32[4,2]{0,1:T(2,128)} %param.25) | copy-start | bytes 100
  56.1 5.9 %copy-start.5 = (f32[1,128,512]{2,0,1:T(1,128)S(1)}, f32[1,128,512]{2,0,1:T(1,128)}, u32[]{:S(2)}) copy-start(f32[1,128,512]{2,0,1:T(1,128)} %get-tuple-element.32) | copy-start | bytes 786436
  56.1 5.9 %copy-start.14 = (s32[128]{0:T(128)S(1)}, s32[128]{0:T(128)}, u32[]{:S(2)}) copy-start(s32[128]{0:T(128)} %param.28) | copy-start | bytes 1540
  56.1 7.2 %copy-start.8 = (f32[128,128]{1,0:T(8,128)S(1)}, f32[128,128]{1,0:T(8,128)}, u32[]{:S(2)}) copy-start(f32[128,128]{1,0:T(8,128)} %param.30) | copy-start | bytes 196612
  59.5 4.7 %copy-start.9 = (f32[1,128,128]{2,1,0:T(8,128)S(1)}, f32[1,128,128]{2,1,0:T(8,128)}, u32[]{:S(2)}) copy-start(f32[1,128,128]{2,1,0:T(8,128)} %param.26) | copy-start | bytes 196612
  60.0 14.5 %collective-permute-start.4 = (f32[128,512]{1,0:T(8,128)S(1)}, f32[128,512]{1,0:T(8,128)S(1)}, u32[]{:S(2)}, u32[]{:S(2)}) collective-permute-start(f32[128,512]{1,0:T(8,128)S(1)} %bitcast.141), channel_id=1, source_target_pairs={{0,1},{1,2},{2,3},{3,4},{4,5},{5,6},{6,7},{7,8},{8,9},{9,10},{10,1... | collective-permute-start | bytes 786440 | tf_op jit(solution)/shard_map/ppermute | solution.py:10
  66.5 11.1 %copy-start.13 = (s32[384]{0:T(512)S(1)}, s32[384]{0:T(512)}, u32[]{:S(2)}) copy-start(s32[384]{0:T(512)} %param.29) | copy-start | bytes 4612
  66.5 19.9 %collective-permute-start.3 = (f32[128,512]{0,1:T(8,128)}, f32[128,512]{0,1:T(8,128)}, u32[]{:S(2)}, u32[]{:S(2)}) collective-permute-start(f32[128,512]{0,1:T(8,128)} %fusion.34), channel_id=1, source_target_pairs={{1,0},{2,1},{3,2},{4,3},{5,4},{6,5},{7,6},{8,7},{9,8},{10,9},{11,1... | collective-permute-start | bytes 786440 | tf_op jit(solution)/shard_map/ppermute | solution.py:10
  74.5 3.5 %copy-start.10 = (f32[128,128]{1,0:T(8,128)S(1)}, f32[128,128]{1,0:T(8,128)}, u32[]{:S(2)}) copy-start(f32[128,128]{1,0:T(8,128)} %param.31) | copy-start | bytes 196612
  83.7 8.0 %collective-permute-start.5 = (f32[128,512]{0,1:T(8,128)}, f32[128,512]{0,1:T(8,128)}, u32[]{:S(2)}, u32[]{:S(2)}) collective-permute-start(f32[128,512]{0,1:T(8,128)} %slice_bitcast_fusion), channel_id=1, source_target_pairs={{1,0},{2,1},{3,2},{4,3},{5,4},{6,5},{7,6},{8,7},{9,8},{10,9},{11,1... | collective-permute-start | bytes 786440 | tf_op jit(solution)/shard_map/ppermute | solution.py:10
  96.3 3.2 %copy-start.4 = (f32[4,2,128,128]{3,2,1,0:T(8,128)S(1)}, f32[4,2,128,128]{3,2,1,0:T(8,128)}, u32[]{:S(2)}) copy-start(f32[4,2,128,128]{3,2,1,0:T(8,128)} %param.24) | copy-start | bytes 1572868
where the time goes:
time: 103 us; the launch traced here: 102 us
  matrix products  41.8 us (41%)
  starting transfers between devices  33.8 us (33%)
  local copies, waits for them, and re-layouts  17.6 us (17%)
  waiting for transfers between devices  5.69 us (6%)
  other arithmetic  3.09 us (3%)
    dot_general x21, matrix products, multiply(): jnp.einsum(formula, left, right, precision=lax.Precision.HIGHEST, preferr...  41.8 us
    ppermute x6, starting transfers between devices, passed_along(): return lax.ppermute(x, axis, pairs)  33.8 us
    dot_general x2, local copies, waits for them, and re-layouts, multiply(): jnp.einsum(formula, left, right, precision=lax.Precision.HIGHEST, preferr...  6.15 us
    ppermute x6, waiting for transfers between devices, passed_along(): return lax.ppermute(x, axis, pairs)  5.69 us
    scatter-add x2, local copies, waits for them, and re-layouts, local(): vector_resid = vector_ext[:vector_count].at[0].add(incoming[1])  2.72 us
    concatenate x1, local copies, waits for them, and re-layouts, local(): vector_extended = jnp.concatenate([vector_fix, returned[1][None]], axis=0)  2.63 us
  transfers between devices with their start and end apart: 6, of which 1 were waited for; matrix products, arithmetic and copies ran while one was open for 34% of the time, Pallas kernels for 0%

commit v1 on v0

v1 whole, which is shorter than its diff:
```python
import jax
import jax.numpy as jnp
from jax import lax
from jax.experimental import pallas as pl
from jax.experimental.pallas import tpu as pltpu
from jax.sharding import PartitionSpec as P

F32 = jnp.float32
BF16 = jnp.bfloat16
B = 128
SLOTS = 6
V_NEXT, NODE, N_NEXT = 3, 4, 5


def crossed(x, pairs):
    return lax.ppermute(x, "region", pairs)


def chip_pairs():
    size = lax.axis_size("region")
    swap = [(i, i ^ 1) for i in range(size)]
    ahead = [(i, i + 1) for i in range(1, size - 1, 2)]
    return swap, ahead, [(b, a) for a, b in ahead]


def is_second():
    return lax.axis_index("region") % 2 == 1


def by_core(first, second):
    pl.when(jnp.logical_not(is_second()))(first)
    pl.when(is_second())(second)


def split(x):
    high = x.astype(BF16)
    return high, (x - high.astype(F32)).astype(BF16)


def left(x):
    high, low = split(x)
    return jnp.concatenate([high, high, low], axis=1)


def right(x):
    high, low = split(x)
    return jnp.concatenate([high, low, high], axis=0)


def mul(x, y):
    return jnp.dot(x, y, preferred_element_type=F32)


def dot3(x, y):
    return mul(left(x), right(y))


def pack(x):
    return jnp.concatenate([x[:64], x[64:]], axis=1)


def unpack(x):
    return jnp.concatenate([x[:, :B], x[:, B:]], axis=0)


def transposed(blocks):
    return left(jnp.concatenate([x.T for x in blocks], axis=0))


def slots_of(gpat, ipat, k):
    return [NODE + gpat[0, k], NODE + gpat[1, k], ipat[0, k], ipat[1, k]]


def send_kernel(gfrom, ifrom, source, smoother, couplings, grad, interp, ahead, swap, gpat, ipat, last, first, mats, pairs, total, sems):
    moves = [
        (source.at[pl.ds(3 * B, B)], last),
        (smoother.at[3], mats.at[0]),
        (couplings.at[3], mats.at[1]),
        (grad.at[3], pairs.at[0]),
        (interp.at[3], pairs.at[1]),
        (gfrom, gpat),
        (ifrom, ipat),
        (source.at[pl.ds(0, B)], first),
        (smoother.at[0], mats.at[2]),
    ]
    copies = [pltpu.make_async_copy(a, b, sems.at[i]) for i, (a, b) in enumerate(moves)]
    for copy in copies:
        copy.start()
    for copy in copies[:3]:
        copy.wait()
    smoothed = dot3(mats[0], last[...])
    ahead[:B] = dot3(mats[1].T, smoothed)
    for copy in copies[3:]:
        copy.wait()

    def first_core():
        swap[...] = ahead[:B]

    def second_core():
        total[...] = jnp.zeros_like(total)
        for s in range(2):
            total[:, :B] += jnp.where(gpat[s, 3] == 1, pairs[0, s], 0.0)
            total[:, B:] += jnp.where(ipat[s, 3] == 3, pairs[1, s], 0.0)
        folded = dot3(total[...].T, mats[1])
        ahead[B:, : 2 * B] = pack(folded[:B])
        ahead[B:, 2 * B :] = pack(folded[B:])
        swap[...] = dot3(mats[2], first[...])

    by_core(first_core, second_core)


def resid_kernel(gpat, ipat, source, smoother, diagonal, couplings, grad, interp, smoothed, held, first_t, last_t):
    held[...] = jnp.zeros_like(held)
    resid = [source[k * B : (k + 1) * B] for k in range(4)]
    for k in range(4):
        got = dot3(smoother[k], source[k * B : (k + 1) * B])
        smoothed[k * B : (k + 1) * B] = got
        rows = [diagonal[k]]
        at = [k]
        if k:
            rows.append(couplings[k - 1])
            at.append(k - 1)
        if k < 3:
            rows.append(couplings[k].T)
            at.append(k + 1)
        terms = mul(left(jnp.concatenate(rows, axis=0)), right(got))
        for i, j in enumerate(at):
            resid[j] = resid[j] - terms[i * B : (i + 1) * B]
    for k in range(4):
        blocks = transposed([grad[k, 0], grad[k, 1], interp[k, 0], interp[k, 1]])
        if k == 0:
            first_t[...] = blocks
        if k == 3:
            last_t[...] = blocks
        terms = mul(blocks, right(resid[k]))
        for i, slot in enumerate(slots_of(gpat, ipat, k)):
            held[slot] += terms[i * B : (i + 1) * B]


def subtract(gpat, ipat, k, blocks, x, target):
    terms = mul(blocks, right(x))
    for i, slot in enumerate(slots_of(gpat, ipat, k)):
        target[slot] -= terms[i * B : (i + 1) * B]


def partial_kernel(gpat, ipat, came, couplings, first_t, last_t, held, out, partial):
    out[...] = held[...]

    def first_core():
        subtract(gpat, ipat, 3, last_t[...], dot3(couplings[3], came[...]), out)

    def second_core():
        subtract(gpat, ipat, 0, first_t[...], came[...], out)
        partial[:B] = out[V_NEXT]
        partial[B:] = out[N_NEXT]

    by_core(first_core, second_core)


def operator_kernel(gpat, ipat, nsm, vsm, nagg, vagg, ncoarse, vcoarse, grad, interp, smoothed, partial, node_op, vec_op, corner, wide, column, behind):
    behind[...] = smoothed[:B]

    def folded(aggregates, coarse):
        width = aggregates.shape[0]
        onehot = (lax.broadcasted_iota(jnp.int32, (B, width), 0) == aggregates[...][None, :]).astype(F32)
        high, low = split(coarse[...])
        pick = onehot.astype(BF16)
        cols = mul(jnp.concatenate([high, low], axis=1), jnp.concatenate([pick, pick], axis=0))
        back = onehot.T.astype(BF16)
        high, low = split(cols)
        return mul(jnp.concatenate([back, back], axis=1), jnp.concatenate([high, low], axis=0))

    n_op = nsm[0] + folded(nagg, ncoarse)
    node_op[...] = left(n_op)
    v_op = folded(vagg, vcoarse)
    zero = jnp.zeros((B, B), F32)
    v_op = v_op + jnp.concatenate(
        [jnp.concatenate([vsm[i] if i == j else zero for j in range(3)], axis=1) for i in range(3)], axis=0
    )
    vec_op[...] = left(v_op)
    corner[:, : 2 * B] = pack(v_op[:B, :B])
    corner[:, 2 * B :] = pack(n_op)
    wide[...] = jnp.zeros_like(wide)
    for k in range(4):
        slots = slots_of(gpat, ipat, k)
        blocks = [grad[k, 0], grad[k, 1], interp[k, 0], interp[k, 1]]
        for slot, block in zip(slots, blocks):
            wide[slot, k * B : (k + 1) * B] += block
    vec = jnp.concatenate([wide[0], wide[1], wide[2]], axis=1)
    column[:, :B] = dot3(vec, v_op[:, :B])
    column[:, B:] = dot3(wide[NODE], n_op)


def fix_all(work, node_op, vec_op, corner, fix, back, full):
    vec = mul(vec_op[...], right(jnp.concatenate([work[0], work[1], work[2]], axis=0)))
    node = mul(node_op[...], right(work[NODE]))
    fix[: 3 * B] = vec
    fix[3 * B :] = node
    back[:B] = vec[:B]
    back[B : 2 * B] = node
    back[2 * B :] = corner[...]
    full[:B] = work[V_NEXT]
    full[B:] = work[N_NEXT]


def first_fix_kernel(gpat, ipat, came, first_t, held, node_op, vec_op, corner, fix, back, full, work):
    def first_core():
        work[...] = held[...]
        subtract(gpat, ipat, 0, first_t[...], came[:B], work)
        fix_all(work, node_op, vec_op, corner, fix, back, full)

    pl.when(jnp.logical_not(is_second()))(first_core)


def second_fix_kernel(gpat, ipat, came, couplings, last_t, held, node_op, vec_op, corner, full_first, fix, full, swap, work):
    def first_core():
        swap[: 2 * B] = full_first[...]

    def second_core():
        work[...] = held[...]
        subtract(gpat, ipat, 3, last_t[...], dot3(couplings[3], came[...]), work)
        fix_all(work, node_op, vec_op, corner, fix, swap, full)

    by_core(first_core, second_core)


def base_kernel(smoothed, fix_first, fix_second, wide, ahead, came, column, out):
    here = [wide[0], wide[1], wide[2], wide[NODE]]

    def first_core():
        mats = ahead[B:]
        folded = jnp.concatenate([unpack(mats[:, 2 * B :]), unpack(mats[:, : 2 * B])], axis=0)
        partial = came[...] - dot3(folded, smoothed[:B])
        blocks = jnp.concatenate([*here, column[...]], axis=1)
        out[...] = smoothed[...] + dot3(blocks, jnp.concatenate([fix_first[...], partial], axis=0))

    def second_core():
        out[...] = smoothed[...] + dot3(jnp.concatenate(here, axis=1), fix_second[...])

    by_core(first_core, second_core)


def next_fix(came, full):
    corner = came[2 * B :]
    vec = came[:B] + dot3(unpack(corner[:, : 2 * B]), full[:B])
    node = came[B : 2 * B] + dot3(unpack(corner[:, 2 * B :]), full[B:])
    return [vec, node]


def last_kernel(came_swap, came_back, full_first, full_second, wide, column, base, out):
    ahead = [wide[V_NEXT], wide[N_NEXT]]

    def first_core():
        rows = next_fix(came_swap, full_first)
        out[...] = base[...] + dot3(jnp.concatenate(ahead, axis=1), jnp.concatenate(rows, axis=0))

    def second_core():
        rows = next_fix(came_back, full_second)
        blocks = jnp.concatenate([*ahead, column[...]], axis=1)
        out[...] = base[...] + dot3(blocks, jnp.concatenate([*rows, came_swap[: 2 * B]], axis=0))

    by_core(first_core, second_core)


VMEM = pl.BlockSpec(memory_space=pltpu.VMEM)
SMEM = pl.BlockSpec(memory_space=pltpu.SMEM)
HBM = pl.BlockSpec(memory_space=pltpu.HBM)
ANY = pl.BlockSpec(memory_space=pl.ANY)


def call(kernel, outs, in_specs, *args, scratch=(), units=0):
    return pl.pallas_call(
        kernel,
        out_shape=[jax.ShapeDtypeStruct(shape, dtype) for shape, dtype in outs],
        in_specs=in_specs,
        out_specs=[VMEM] * len(outs),
        scratch_shapes=list(scratch),
        compiler_params=pltpu.CompilerParams(vmem_limit_bytes=24 * 1024 * 1024),
        cost_estimate=pl.CostEstimate(flops=units * 50331648, bytes_accessed=units, transcendentals=0),
    )(*args)


def local(
    right_side,
    smoother,
    diagonal_blocks,
    couplings,
    grad_blocks,
    grad_pattern,
    interp_blocks,
    interp_pattern,
    node_smoother,
    vector_smoother,
    node_aggregates,
    vector_aggregates,
    node_coarse,
    vector_coarse,
):
    vectors = right_side.shape[1]
    pats = (grad_pattern.T, interp_pattern.T)

    swap, ahead, behind = chip_pairs()

    sent_ahead, sent_swap = call(
        send_kernel,
        [((B + 64, vectors), F32), ((B, vectors), F32)],
        [HBM] * 7,
        *(
            pltpu.with_memory_space_constraint(x, pltpu.HBM)
            for x in (*pats, right_side, smoother, couplings, grad_blocks, interp_blocks)
        ),
        scratch=[
            pltpu.SMEM((2, 4), jnp.int32),
            pltpu.SMEM((2, 4), jnp.int32),
            pltpu.VMEM((B, vectors), F32),
            pltpu.VMEM((B, vectors), F32),
            pltpu.VMEM((3, B, B), F32),
            pltpu.VMEM((2, 2, B, B), F32),
            pltpu.VMEM((B, 2 * B), F32),
            pltpu.SemaphoreType.DMA((9,)),
        ],
    )
    came_ahead = crossed(sent_ahead, ahead)
    came_swap = crossed(sent_swap, swap)

    smoothed, held, first_t, last_t = call(
        resid_kernel,
        [((4 * B, vectors), F32), ((SLOTS, B, vectors), F32), ((4 * B, 3 * B), BF16), ((4 * B, 3 * B), BF16)],
        [SMEM] * 2 + [VMEM] * 6,
        *pats, right_side, smoother, diagonal_blocks, couplings, grad_blocks, interp_blocks,
        units=30,
    )
    held, partial = call(
        partial_kernel,
        [((SLOTS, B, vectors), F32), ((2 * B, vectors), F32)],
        [SMEM] * 2 + [VMEM] * 5,
        *pats, came_swap, couplings, first_t, last_t, held,
        units=0,
    )
    came_partial = crossed(partial, ahead)

    node_op, vec_op, corner, wide, column, sent_behind = call(
        operator_kernel,
        [
            ((B, 3 * B), BF16),
            ((3 * B, 9 * B), BF16),
            ((64, vectors), F32),
            ((SLOTS, 4 * B, B), F32),
            ((4 * B, 2 * B), F32),
            ((B, vectors), F32),
        ],
        [SMEM] * 2 + [VMEM] * 9 + [ANY],
        *pats, node_smoother, vector_smoother, node_aggregates, vector_aggregates,
        node_coarse, vector_coarse, grad_blocks, interp_blocks, smoothed, partial,
        units=0,
    )
    came_behind = crossed(sent_behind, behind)
    sizes = [((4 * B, vectors), F32), ((2 * B + 64, vectors), F32), ((2 * B, vectors), F32)]
    work = [pltpu.VMEM((SLOTS, B, vectors), F32)]
    fix_first, sent_back, full_first = call(
        first_fix_kernel,
        sizes,
        [SMEM] * 2 + [VMEM] * 6,
        *pats, came_ahead, first_t, held, node_op, vec_op, corner,
        scratch=work,
        units=100,
    )
    came_back = crossed(sent_back, behind)
    fix_second, full_second, sent_swap = call(
        second_fix_kernel,
        [sizes[0], sizes[2], sizes[1]],
        [SMEM] * 2 + [VMEM] * 8,
        *pats, came_behind, couplings, last_t, held, node_op, vec_op, corner, full_first,
        scratch=work,
        units=0,
    )
    came_swap = crossed(sent_swap, swap)
    (base,) = call(
        base_kernel,
        [((4 * B, vectors), F32)],
        [VMEM] * 7,
        smoothed, fix_first, fix_second, wide, came_ahead, came_partial, column,
        units=60,
    )
    (out,) = call(
        last_kernel,
        [((4 * B, vectors), F32)],
        [VMEM] * 7,
        came_swap, came_back, full_first, full_second, wide, column, base,
    )
    return out


def solution(mesh):
    in_specs = (
        P("region", None),
        P("region", None, None),
        P("region", None, None),
        P("region", None, None),
        P("region", None, None, None),
        P("region", None),
        P("region", None, None, None),
        P("region", None),
        P("region", None, None),
        P("region", None, None),
        P("region"),
        P("region"),
        P("region", None),
        P("region", None),
    )
    out_specs = P("region", None)
    return jax.shard_map(local, mesh=mesh, in_specs=in_specs, out_specs=out_specs, check_vma=False)
```

time: 103 us -> 45.1 us (0.44)
  matrix products: 41.8 us -> 0 us
  local copies, waits for them, and re-layouts: 17.6 us -> 1.01 us
  Pallas kernels: 0 us -> 14.2 us
  starting transfers between devices: 33.8 us -> 25.5 us
  other arithmetic: 3.09 us -> 0 us
  waiting for transfers between devices: 5.69 us -> 3.87 us
    dot_general x21 -> x0, matrix products: 41.8 us -> none  [multiply(): jnp.einsum(formula, left, right, precision=lax.Precision.HIGHEST, preferr...]
    pallas_call x0 -> x8, Pallas kernels: none -> 14.2 us  [call(): pl.pallas_call(kernel, out_shape=[jax.ShapeDtypeStruct(shape, dtype) for...]
    ppermute x6, starting transfers between devices: 33.8 us -> 25.5 us  [crossed(): return lax.ppermute(x, 'region', pairs)]
    dot_general x2 -> x0, local copies, waits for them, and re-layouts: 6.15 us -> none  [multiply(): jnp.einsum(formula, left, right, precision=lax.Precision.HIGHEST, preferr...]
    concatenate x2 -> x0, other arithmetic: 3.05 us -> none  [the longest x1 1.99 us: local(): vector_extended = jnp.concatenate([vector_fix, returned[1][None]], axis=0)]
    concatenate x2 -> x0, local copies, waits for them, and re-layouts: 2.86 us -> none  [the longest x1 2.63 us: local(): vector_extended = jnp.concatenate([vector_fix, returned[1][None]], axis=0)]
    scatter-add x2 -> x0, local copies, waits for them, and re-layouts: 2.72 us -> none  [local(): vector_resid = vector_ext[:vector_count].at[0].add(incoming[1])]
    reshape x2 -> x0, local copies, waits for them, and re-layouts: 2.46 us -> none  [the longest x1 1.31 us: local(): source = right_side.reshape(blocks_here, width, vectors)]
  transfers between devices with their start and end apart: 6 -> 6, of which waited for: 1 -> 2; matrix products, arithmetic and copies ran while one was open for 34% -> 0% of each run, Pallas kernels for 0% -> 24%
where the time goes in v1:
time: 45.1 us; the launch traced here: 44.9 us
  starting transfers between devices  25.5 us (57%)
  Pallas kernels  14.2 us (31%)
  waiting for transfers between devices  3.87 us (9%)
  local copies, waits for them, and re-layouts  1.01 us (2%)
    ppermute x6, starting transfers between devices, crossed(): return lax.ppermute(x, 'region', pairs)  25.5 us
    pallas_call x8, Pallas kernels, call(): pl.pallas_call(kernel, out_shape=[jax.ShapeDtypeStruct(shape, dtype) for...  14.2 us
    ppermute x6, waiting for transfers between devices, crossed(): return lax.ppermute(x, 'region', pairs)  3.87 us
    unnamed x28, local copies, waits for them, and re-layouts  1.01 us
  transfers between devices with their start and end apart: 6, of which 2 were waited for; matrix products, arithmetic and copies ran while one was open for 0% of the time, Pallas kernels for 24%

profile of v1, /device:TPU:6, one launch (start us, length us, event | category | flops | bytes accessed | tf_op | source)
XLA Modules:
  0.0 44.9 jit_solution(2079778315442405423)
XLA Ops:
  0.0 0.0 copy-start
  0.0 0.0 copy-start.2
  0.0 0.0 copy-start.1
  0.0 0.0 copy-start.4
  0.0 0.0 copy-start.3
  0.0 0.0 copy-start.10
  0.0 0.0 copy-start.9
  0.0 1.7 %shard_map.137 = (f32[192,512]{1,0:T(8,128)S(1)}, f32[128,512]{1,0:T(8,128)S(1)}) custom-call(s32[2,4]{1,0:T(2,128)} %bitcast.2, s32[2,4]{1,0:T(2,128)} %bitcast.8, f32[512,512]{1,0:T(8,128)} %source.3, f32[4,128,128]{2,1,0:T(8,128)} %smoother.3, f32[4,128,128]{2,1,0:T(8,128)} %couplings.7, f32[4,2,128,128]{3,2,1,0:T(8,128)} %grad.5, f32[4,2,128,128]{3,2,1,0:T(8,128)} %interp.5), custom_call_target="tpu_custom_call" | custom-call | tf_op jit(solution)/shard_map/pallas_call | solution.py:272
  1.8 1.3 %collective-permute-start.2 = (f32[192,512]{1,0:T(8,128)S(1)}, f32[192,512]{1,0:T(8,128)S(1)}, u32[]{:S(2)}, u32[]{:S(2)}) collective-permute-start(f32[192,512]{1,0:T(8,128)S(1)} %get-tuple-element.36), channel_id=1, source_target_pairs={{1,2},{3,4},{5,6},{7,8},{9,10},{11,12},{13,14},{15,16},{17,18},{19... | collective-permute-start | bytes 1179656 | tf_op jit(solution)/shard_map/ppermute | solution.py:16
  3.1 4.2 %collective-permute-start = (f32[128,512]{1,0:T(8,128)S(1)}, f32[128,512]{1,0:T(8,128)S(1)}, u32[]{:S(2)}, u32[]{:S(2)}) collective-permute-start(f32[128,512]{1,0:T(8,128)S(1)} %get-tuple-element.26), channel_id=1, source_target_pairs={{0,1},{1,0},{2,3},{3,2},{4,5},{5,4},{6,7},{7,6},{8,9},{9,8},{10,11... | collective-permute-start | bytes 786440 | tf_op jit(solution)/shard_map/ppermute | solution.py:16
  7.3 0.0 copy-done
  7.3 0.0 copy-done.2
  7.3 0.0 copy-done.1
  7.3 0.0 copy-done.4
  7.3 0.0 copy-done.3
  7.4 0.0 copy-done.10
  7.4 0.0 copy-done.9
  7.4 0.0 copy-start.13
  7.4 0.9 %copy-done.13 = f32[4,128,128]{2,1,0:T(8,128)S(1)} copy-done((f32[4,128,128]{2,1,0:T(8,128)S(1)}, f32[4,128,128]{2,1,0:T(8,128)}, u32[]{:S(2)}) %copy-start.13) | copy-done | bytes 262168
  8.3 3.5 %shard_map.136 = (f32[512,512]{1,0:T(8,128)S(1)}, f32[6,128,512]{2,1,0:T(8,128)S(1)}, bf16[512,384]{1,0:T(8,128)(2,1)S(1)}, bf16[512,384]{1,0:T(8,128)(2,1)S(1)}) custom-call(s32[2,4]{1,0:T(2,128)S(1)} %bitcast.3, s32[2,4]{1,0:T(2,128)S(1)} %bitcast.9, f32[512,512]{1,0:T(8,128)S(1)} %copy-done.3, f32[4,128,128]{2,1,0:T(8,128)S(1)} %copy-done.4, ...), custom_call_target="tpu_custom_call" | custom-call | flops 1509949440 | bytes 30 | tf_op jit(solution)/shard_map/pallas_call | solution.py:272
  11.9 0.0 copy-start.5
  11.9 0.0 copy-start.6
  11.9 0.0 copy-start.7
  11.9 0.0 copy-start.8
  11.9 0.0 copy-start.11
  11.9 0.0 copy-start.12
  11.9 0.0 collective-permute-done.came
  11.9 1.3 %shard_map.138 = (f32[6,128,512]{2,1,0:T(8,128)S(1)}, f32[256,512]{1,0:T(8,128)S(1)}) custom-call(s32[2,4]{1,0:T(2,128)S(1)} %bitcast.4, s32[2,4]{1,0:T(2,128)S(1)} %bitcast.10, f32[128,512]{1,0:T(8,128)S(1)} %collective-permute-done.came, f32[4,128,128]{2,1,0:T(8,128)S(1)} %copy-done, bf16[512,384]{1,0:T(8,128)(2,1)S(1)} %get-tuple-element.27.first_t, ...), custom_call_target="tpu_custom_call" | custom-call | tf_op jit(solution)/shard_map/pallas_call | solution.py:272
  13.3 1.3 %collective-permute-start.5 = (f32[256,512]{1,0:T(8,128)S(1)}, f32[256,512]{1,0:T(8,128)S(1)}, u32[]{:S(2)}, u32[]{:S(2)}) collective-permute-start(f32[256,512]{1,0:T(8,128)S(1)} %get-tuple-element.30.partial), channel_id=1, source_target_pairs={{1,2},{3,4},{5,6},{7,8},{9,10},{11,12},{13,14},{15,16},{17,18},{19... | collective-permute-start | bytes 1572872 | tf_op jit(solution)/shard_map/ppermute | solution.py:16
  14.6 0.0 copy-done.5
  14.6 0.0 copy-done.6
  14.6 0.0 copy-done.7
  14.6 0.0 copy-done.8
  14.6 0.0 copy-done.11
  14.6 0.0 copy-done.12
  14.6 1.7 %shard_map.139 = (bf16[128,384]{1,0:T(8,128)(2,1)S(1)}, bf16[384,1152]{1,0:T(8,128)(2,1)S(1)}, f32[64,512]{1,0:T(8,128)S(1)}, f32[6,512,128]{2,1,0:T(8,128)S(1)}...) custom-call(s32[2,4]{1,0:T(2,128)S(1)} %bitcast.5, s32[2,4]{1,0:T(2,128)S(1)} %bitcast.11, f32[1,128,128]{2,1,0:T(8,128)S(1)} %copy-done.6, ...), custom_call_target="tpu_custom_call" | custom-call | tf_op jit(solution)/shard_map/pallas_call | solution.py:272
  16.4 15.4 %collective-permute-start.1 = (f32[128,512]{1,0:T(8,128)S(1)}, f32[128,512]{1,0:T(8,128)S(1)}, u32[]{:S(2)}, u32[]{:S(2)}) collective-permute-start(f32[128,512]{1,0:T(8,128)S(1)} %get-tuple-element.31), channel_id=1, source_target_pairs={{2,1},{4,3},{6,5},{8,7},{10,9},{12,11},{14,13},{16,15},{18,17},{20... | collective-permute-start | bytes 786440 | tf_op jit(solution)/shard_map/ppermute | solution.py:16
  31.8 0.0 collective-permute-done.2.came.ahead
  31.8 1.8 %shard_map.140 = (f32[512,512]{1,0:T(8,128)S(1)}, f32[320,512]{1,0:T(8,128)S(1)}, f32[256,512]{1,0:T(8,128)S(1)}) custom-call(s32[2,4]{1,0:T(2,128)S(1)} %bitcast.6, s32[2,4]{1,0:T(2,128)S(1)} %bitcast.12, f32[192,512]{1,0:T(8,128)S(1)} %collective-permute-done.2.came.ahead, bf16[512,384]{1,0:T(8,128)(2,1)S(1)} %get-tuple-element.27.first_t, ...), custom_call_target="tpu_custom_call" | custom-call | flops 5033164800 | bytes 100 | tf_op jit(solution)/shard_map/pallas_call | solution.py:272
  33.6 1.3 %collective-permute-start.4 = (f32[320,512]{1,0:T(8,128)S(1)}, f32[320,512]{1,0:T(8,128)S(1)}, u32[]{:S(2)}, u32[]{:S(2)}) collective-permute-start(f32[320,512]{1,0:T(8,128)S(1)} %get-tuple-element.39), channel_id=1, source_target_pairs={{2,1},{4,3},{6,5},{8,7},{10,9},{12,11},{14,13},{16,15},{18,17},{20... | collective-permute-start | bytes 1966088 | tf_op jit(solution)/shard_map/ppermute | solution.py:16
  34.9 0.7 %collective-permute-done.1.came = f32[128,512]{1,0:T(8,128)S(1)} collective-permute-done((f32[128,512]{1,0:T(8,128)S(1)}, f32[128,512]{1,0:T(8,128)S(1)}, u32[]{:S(2)}, u32[]{:S(2)}) %collective-permute-start.1) | collective-permute-done | bytes 262176 | tf_op jit(solution)/shard_map/ppermute | solution.py:16
  35.6 0.6 %shard_map.141 = (f32[512,512]{1,0:T(8,128)S(1)}, f32[256,512]{1,0:T(8,128)S(1)}, f32[320,512]{1,0:T(8,128)S(1)}) custom-call(s32[2,4]{1,0:T(2,128)S(1)} %bitcast.7, s32[2,4]{1,0:T(2,128)S(1)} %bitcast.13, f32[128,512]{1,0:T(8,128)S(1)} %collective-permute-done.1.came, f32[4,128,128]{2,1,0:T(8,128)S(1)} %copy-done, ...), custom_call_target="tpu_custom_call" | custom-call | tf_op jit(solution)/shard_map/pallas_call | solution.py:272
  36.2 1.9 %collective-permute-start.3 = (f32[320,512]{1,0:T(8,128)S(1)}, f32[320,512]{1,0:T(8,128)S(1)}, u32[]{:S(2)}, u32[]{:S(2)}) collective-permute-start(f32[320,512]{1,0:T(8,128)S(1)} %get-tuple-element.38), channel_id=1, source_target_pairs={{0,1},{1,0},{2,3},{3,2},{4,5},{5,4},{6,7},{7,6},{8,9},{9,8},{10,11... | collective-permute-start | bytes 1966088 | tf_op jit(solution)/shard_map/ppermute | solution.py:16
  38.2 0.0 collective-permute-done.5.came
  38.2 1.6 %shard_map.142.base = f32[512,512]{1,0:T(8,128)S(1)} custom-call(f32[512,512]{1,0:T(8,128)S(1)} %get-tuple-element.25.smoothed, f32[512,512]{1,0:T(8,128)S(1)} %get-tuple-element.43.fix_first, f32[512,512]{1,0:T(8,128)S(1)} %get-tuple-element.44.fix_second, f32[6,512,128]{2,1,0:T(8,128)S(1)} %get-tuple-element.41.wide, ...), custom_call_target="tpu_custom_call" | custom-call | flops 3019898880 | bytes 60 | tf_op jit(solution)/shard_map/pallas_call | solution.py:272
  39.8 3.2 %collective-permute-done.4.came_back = f32[320,512]{1,0:T(8,128)S(1)} collective-permute-done((f32[320,512]{1,0:T(8,128)S(1)}, f32[320,512]{1,0:T(8,128)S(1)}, u32[]{:S(2)}, u32[]{:S(2)}) %collective-permute-start.4) | collective-permute-done | bytes 655392 | tf_op jit(solution)/shard_map/ppermute | solution.py:16
  43.0 0.0 collective-permute-done.3.came_swap
  43.0 1.9 %shard_map.143 = f32[512,512]{1,0:T(8,128)} custom-call(f32[320,512]{1,0:T(8,128)S(1)} %collective-permute-done.3.came_swap, f32[320,512]{1,0:T(8,128)S(1)} %collective-permute-done.4.came_back, f32[256,512]{1,0:T(8,128)S(1)} %get-tuple-element.37.full_first, f32[256,512]{1,0:T(8,128)S(1)} %get-tuple-element.40.full_second, ...), custom_call_target="tpu_custom_call" | custom-call | tf_op jit(solution)/shard_map/pallas_call | solution.py:272
Async XLA Ops:
  0.0 7.3 %copy-start = (f32[4,128,128]{2,1,0:T(8,128)S(1)}, f32[4,128,128]{2,1,0:T(8,128)}, u32[]{:S(2)}) copy-start(f32[4,128,128]{2,1,0:T(8,128)} %couplings.7) | copy-start | bytes 786436
  0.0 7.3 %copy-start.2 = (f32[4,2,128,128]{3,2,1,0:T(8,128)S(1)}, f32[4,2,128,128]{3,2,1,0:T(8,128)}, u32[]{:S(2)}) copy-start(f32[4,2,128,128]{3,2,1,0:T(8,128)} %interp.5) | copy-start | bytes 1572868
  0.0 7.3 %copy-start.1 = (f32[4,2,128,128]{3,2,1,0:T(8,128)S(1)}, f32[4,2,128,128]{3,2,1,0:T(8,128)}, u32[]{:S(2)}) copy-start(f32[4,2,128,128]{3,2,1,0:T(8,128)} %grad.5) | copy-start | bytes 1572868
  0.0 7.3 %copy-start.4 = (f32[4,128,128]{2,1,0:T(8,128)S(1)}, f32[4,128,128]{2,1,0:T(8,128)}, u32[]{:S(2)}) copy-start(f32[4,128,128]{2,1,0:T(8,128)} %smoother.3) | copy-start | bytes 786436
  0.0 7.3 %copy-start.3 = (f32[512,512]{1,0:T(8,128)S(1)}, f32[512,512]{1,0:T(8,128)}, u32[]{:S(2)}) copy-start(f32[512,512]{1,0:T(8,128)} %source.3) | copy-start | bytes 3145732
  0.0 7.3 %copy-start.10 = (s32[4,2]{0,1:T(2,128)S(1)}, s32[4,2]{0,1:T(2,128)}, u32[]{:S(2)}) copy-start(s32[4,2]{0,1:T(2,128)} %param.21) | copy-start | bytes 100
  0.0 7.3 %copy-start.9 = (s32[4,2]{0,1:T(2,128)S(1)}, s32[4,2]{0,1:T(2,128)}, u32[]{:S(2)}) copy-start(s32[4,2]{0,1:T(2,128)} %param.19) | copy-start | bytes 100
  1.8 30.0 %collective-permute-start.2 = (f32[192,512]{1,0:T(8,128)S(1)}, f32[192,512]{1,0:T(8,128)S(1)}, u32[]{:S(2)}, u32[]{:S(2)}) collective-permute-start(f32[192,512]{1,0:T(8,128)S(1)} %get-tuple-element.36), channel_id=1, source_target_pairs={{1,2},{3,4},{5,6},{7,8},{9,10},{11,12},{13,14},{15,16},{17,18},{19... | collective-permute-start | bytes 1179656 | tf_op jit(solution)/shard_map/ppermute | solution.py:16
  3.1 8.9 %collective-permute-start = (f32[128,512]{1,0:T(8,128)S(1)}, f32[128,512]{1,0:T(8,128)S(1)}, u32[]{:S(2)}, u32[]{:S(2)}) collective-permute-start(f32[128,512]{1,0:T(8,128)S(1)} %get-tuple-element.26), channel_id=1, source_target_pairs={{0,1},{1,0},{2,3},{3,2},{4,5},{5,4},{6,7},{7,6},{8,9},{9,8},{10,11... | collective-permute-start | bytes 786440 | tf_op jit(solution)/shard_map/ppermute | solution.py:16
  7.4 1.0 %copy-start.13 = (f32[4,128,128]{2,1,0:T(8,128)S(1)}, f32[4,128,128]{2,1,0:T(8,128)}, u32[]{:S(2)}) copy-start(f32[4,128,128]{2,1,0:T(8,128)} %diagonal.1) | copy-start | bytes 786436
  11.9 2.7 %copy-start.5 = (f32[3,128,128]{2,1,0:T(8,128)S(1)}, f32[3,128,128]{2,1,0:T(8,128)}, u32[]{:S(2)}) copy-start(f32[3,128,128]{2,1,0:T(8,128)} %vsm.1) | copy-start | bytes 589828
  11.9 2.7 %copy-start.6 = (f32[1,128,128]{2,1,0:T(8,128)S(1)}, f32[1,128,128]{2,1,0:T(8,128)}, u32[]{:S(2)}) copy-start(f32[1,128,128]{2,1,0:T(8,128)} %nsm.1) | copy-start | bytes 196612
  11.9 2.7 %copy-start.7 = (f32[128,128]{1,0:T(8,128)S(1)}, f32[128,128]{1,0:T(8,128)}, u32[]{:S(2)}) copy-start(f32[128,128]{1,0:T(8,128)} %ncoarse.1) | copy-start | bytes 196612
  11.9 2.7 %copy-start.8 = (f32[128,128]{1,0:T(8,128)S(1)}, f32[128,128]{1,0:T(8,128)}, u32[]{:S(2)}) copy-start(f32[128,128]{1,0:T(8,128)} %vcoarse.1) | copy-start | bytes 196612
  11.9 2.7 %copy-start.11 = (s32[384]{0:T(512)S(1)}, s32[384]{0:T(512)}, u32[]{:S(2)}) copy-start(s32[384]{0:T(512)} %vagg.1) | copy-start | bytes 4612
  11.9 2.7 %copy-start.12 = (s32[128]{0:T(128)S(1)}, s32[128]{0:T(128)}, u32[]{:S(2)}) copy-start(s32[128]{0:T(128)} %nagg.1) | copy-start | bytes 1540
  13.3 24.9 %collective-permute-start.5 = (f32[256,512]{1,0:T(8,128)S(1)}, f32[256,512]{1,0:T(8,128)S(1)}, u32[]{:S(2)}, u32[]{:S(2)}) collective-permute-start(f32[256,512]{1,0:T(8,128)S(1)} %get-tuple-element.30.partial), channel_id=1, source_target_pairs={{1,2},{3,4},{5,6},{7,8},{9,10},{11,12},{13,14},{15,16},{17,18},{19... | collective-permute-start | bytes 1572872 | tf_op jit(solution)/shard_map/ppermute | solution.py:16
  16.4 19.3 %collective-permute-start.1 = (f32[128,512]{1,0:T(8,128)S(1)}, f32[128,512]{1,0:T(8,128)S(1)}, u32[]{:S(2)}, u32[]{:S(2)}) collective-permute-start(f32[128,512]{1,0:T(8,128)S(1)} %get-tuple-element.31), channel_id=1, source_target_pairs={{2,1},{4,3},{6,5},{8,7},{10,9},{12,11},{14,13},{16,15},{18,17},{20... | collective-permute-start | bytes 786440 | tf_op jit(solution)/shard_map/ppermute | solution.py:16
  33.6 9.4 %collective-permute-start.4 = (f32[320,512]{1,0:T(8,128)S(1)}, f32[320,512]{1,0:T(8,128)S(1)}, u32[]{:S(2)}, u32[]{:S(2)}) collective-permute-start(f32[320,512]{1,0:T(8,128)S(1)} %get-tuple-element.39), channel_id=1, source_target_pairs={{2,1},{4,3},{6,5},{8,7},{10,9},{12,11},{14,13},{16,15},{18,17},{20... | collective-permute-start | bytes 1966088 | tf_op jit(solution)/shard_map/ppermute | solution.py:16
  36.2 6.7 %collective-permute-start.3 = (f32[320,512]{1,0:T(8,128)S(1)}, f32[320,512]{1,0:T(8,128)S(1)}, u32[]{:S(2)}, u32[]{:S(2)}) collective-permute-start(f32[320,512]{1,0:T(8,128)S(1)} %get-tuple-element.38), channel_id=1, source_target_pairs={{0,1},{1,0},{2,3},{3,2},{4,5},{5,4},{6,7},{7,6},{8,9},{9,8},{10,11... | collective-permute-start | bytes 1966088 | tf_op jit(solution)/shard_map/ppermute | solution.py:16

commit v2 on v1

v2 whole, which is shorter than its diff:
```python
import jax
import jax.numpy as jnp
from jax import lax
from jax.experimental import pallas as pl
from jax.experimental.pallas import tpu as pltpu
from jax.sharding import PartitionSpec as P

F32 = jnp.float32
BF16 = jnp.bfloat16
B = 128
SLOTS = 6
V_NEXT, NODE, N_NEXT = 3, 4, 5


def crossed(x, pairs):
    return lax.ppermute(x, "region", pairs)


def chip_pairs():
    size = lax.axis_size("region")
    swap = [(i, i ^ 1) for i in range(size)]
    ahead = [(i, i + 1) for i in range(1, size - 1, 2)]
    return swap, ahead, [(b, a) for a, b in ahead]


def is_second():
    return lax.axis_index("region") % 2 == 1


def by_core(first, second):
    pl.when(jnp.logical_not(is_second()))(first)
    pl.when(is_second())(second)


def split(x):
    high = x.astype(BF16)
    return high, (x - high.astype(F32)).astype(BF16)


def left(x):
    high, low = split(x)
    return jnp.concatenate([high, high, low], axis=1)


def right(x):
    high, low = split(x)
    return jnp.concatenate([high, low, high], axis=0)


def mul(x, y):
    return jnp.dot(x, y, preferred_element_type=F32)


def dot3(x, y):
    return mul(left(x), right(y))


def pack(x):
    return jnp.concatenate([x[:64], x[64:]], axis=1)


def unpack(x):
    return jnp.concatenate([x[:, :B], x[:, B:]], axis=0)


def transposed(blocks):
    return left(jnp.concatenate([x.T for x in blocks], axis=0))


def slots_of(gpat, ipat, k):
    return [NODE + gpat[0, k], NODE + gpat[1, k], ipat[0, k], ipat[1, k]]


def fetched(gfrom, ifrom, gpat, ipat, sems):
    copies = [pltpu.make_async_copy(gfrom, gpat, sems.at[0]), pltpu.make_async_copy(ifrom, ipat, sems.at[1])]
    for copy in copies:
        copy.start()
    return copies


def wait_all(copies):
    for copy in copies:
        copy.wait()


def named(pattern, s, k, block, value):
    return jnp.where(pattern[s : s + 1, k : k + 1] == value, block, 0.0)


def send_kernel(
    gfrom, ifrom, source, smoother, couplings, grad, interp, diagonal_from, ahead, swap, diagonal,
    gpat, ipat, last, first, mats, pairs, total, sems
):
    moves = [
        (source.at[pl.ds(3 * B, B)], last),
        (smoother.at[3], mats.at[0]),
        (couplings.at[3], mats.at[1]),
        (grad.at[3], pairs.at[0]),
        (interp.at[3], pairs.at[1]),
        (gfrom, gpat),
        (ifrom, ipat),
        (source.at[pl.ds(0, B)], first),
        (smoother.at[0], mats.at[2]),
        (diagonal_from, diagonal),
    ]
    copies = [pltpu.make_async_copy(a, b, sems.at[i]) for i, (a, b) in enumerate(moves)]
    for copy in copies:
        copy.start()
    wait_all(copies[:-1])
    smoothed = dot3(mats[0], last[...])
    beside = dot3(mats[2], first[...])
    total[...] = jnp.zeros_like(total)
    for s in range(2):
        total[:, :B] += named(gpat, s, 3, pairs[0, s], 1)
        total[:, B:] += named(ipat, s, 3, pairs[1, s], 3)
    folded = dot3(total[...].T, mats[1])
    ahead[B:, : 2 * B] = pack(folded[:B])
    ahead[B:, 2 * B :] = pack(folded[B:])
    onward = dot3(mats[1].T, smoothed)
    ahead[:B] = onward
    swap[...] = jnp.where(is_second(), beside, onward)
    copies[-1].wait()


def resid_kernel(gpat, ipat, source, smoother, diagonal, couplings, grad, interp, smoothed, resid, named_next, total):
    for k in range(4):
        smoothed[k * B : (k + 1) * B] = dot3(smoother[k], source[k * B : (k + 1) * B])
        rows = slice(k * B, (k + 1) * B)
        total[rows, :B] = sum(named(ipat, s, k, interp[k, s], 3) for s in range(2))
        total[rows, B:] = sum(named(gpat, s, k, grad[k, s], 1) for s in range(2))
    named_next[...] = left(total[...].T)
    zero = jnp.zeros((B, B), F32)
    rows = []
    for k in range(4):
        row = [zero] * 4
        row[k] = diagonal[k]
        if k:
            row[k - 1] = couplings[k - 1].T
        if k < 3:
            row[k + 1] = couplings[k]
        rows.append(jnp.concatenate(row, axis=1))
    resid[...] = source[...] - mul(left(jnp.concatenate(rows, axis=0)), right(smoothed[...]))


def partial_kernel(came, resid, named_next, partial):
    def second_core():
        whole = jnp.concatenate([resid[:B] - came[...], resid[B:]], axis=0)
        partial[...] = mul(named_next[...], right(whole))

    pl.when(is_second())(second_core)


def subtract(gpat, ipat, k, blocks, x, target, pats=()):
    terms = mul(blocks, right(x))
    wait_all(pats)
    for i, slot in enumerate(slots_of(gpat, ipat, k)):
        target[slot] -= terms[i * B : (i + 1) * B]


def operators(gpat, ipat, nsm, vsm, nagg, vagg, ncoarse, vcoarse, grad, interp, node_op, vec_op, corner, wide, column):
    def folded(aggregates, coarse):
        width = aggregates.shape[0]
        onehot = (lax.broadcasted_iota(jnp.int32, (B, width), 0) == aggregates[...][None, :]).astype(F32)
        high, low = split(coarse[...])
        pick = onehot.astype(BF16)
        cols = mul(jnp.concatenate([high, low], axis=1), jnp.concatenate([pick, pick], axis=0))
        back = onehot.T.astype(BF16)
        high, low = split(cols)
        return mul(jnp.concatenate([back, back], axis=1), jnp.concatenate([high, low], axis=0))

    n_op = nsm[0] + folded(nagg, ncoarse)
    node_op[...] = left(n_op)
    v_op = folded(vagg, vcoarse)
    zero = jnp.zeros((B, B), F32)
    v_op = v_op + jnp.concatenate(
        [jnp.concatenate([vsm[i] if i == j else zero for j in range(3)], axis=1) for i in range(3)], axis=0
    )
    vec_op[...] = left(v_op)
    corner[:, : 2 * B] = pack(v_op[:B, :B])
    corner[:, 2 * B :] = pack(n_op)
    wide[...] = jnp.zeros_like(wide)
    for k in range(4):
        slots = slots_of(gpat, ipat, k)
        blocks = [grad[k, 0], grad[k, 1], interp[k, 0], interp[k, 1]]
        for slot, block in zip(slots, blocks):
            wide[slot, k * B : (k + 1) * B] += block
    vec = jnp.concatenate([wide[0], wide[1], wide[2]], axis=1)
    column[:, :B] = dot3(vec, v_op[:, :B])
    column[:, B:] = dot3(wide[NODE], n_op)


def fix_all(work, node_op, vec_op, corner, fix, back, full):
    vec = mul(vec_op[...], right(jnp.concatenate([work[0], work[1], work[2]], axis=0)))
    node = mul(node_op[...], right(work[NODE]))
    fix[: 3 * B] = vec
    fix[3 * B :] = node
    back[:B] = vec[:B]
    back[B : 2 * B] = node
    back[2 * B : 2 * B + 64] = corner[...]
    full[:B] = work[V_NEXT]
    full[B:] = work[N_NEXT]


def prepare(keep, gfrom, ifrom, *refs):
    mats, (resid, came, couplings), outs = refs[:8], refs[8:11], refs[12:]
    node_op, vec_op, corner, wide, column, held, kept, gpat, ipat, sems = outs
    grad, interp = mats[6:]
    wait_all(fetched(gfrom, ifrom, gpat, ipat, sems))
    operators(gpat, ipat, *mats, node_op, vec_op, corner, wide, column)
    held[...] = jnp.zeros_like(held)
    for k in range(4):
        blocks = transposed([grad[k, 0], grad[k, 1], interp[k, 0], interp[k, 1]])
        if k == keep:
            kept[...] = blocks
        rows = resid[k * B : (k + 1) * B]
        if keep == 0 and k == 3:
            rows = rows - dot3(couplings[3], came[...])
        if keep == 3 and k == 0:
            rows = rows - came[...]
        terms = mul(blocks, right(rows))
        for i, slot in enumerate(slots_of(gpat, ipat, k)):
            held[slot] += terms[i * B : (i + 1) * B]


def first_prepare_kernel(*refs):
    pl.when(jnp.logical_not(is_second()))(lambda: prepare(0, *refs))


def second_prepare_kernel(*refs):
    pl.when(is_second())(lambda: prepare(3, *refs))


def first_fix_kernel(
    gfrom, ifrom, came, first_t, held, node_op, vec_op, corner, smoothed, fix, back, full, behind, gpat, ipat, sems, work
):
    def first_core():
        pats = fetched(gfrom, ifrom, gpat, ipat, sems)
        behind[...] = smoothed[:B]
        work[...] = held[...]
        subtract(gpat, ipat, 0, first_t[...], came[:B], work, pats)
        fix_all(work, node_op, vec_op, corner, fix, back, full)

    pl.when(jnp.logical_not(is_second()))(first_core)


def second_fix_kernel(
    gfrom, ifrom, came, couplings, last_t, held, node_op, vec_op, corner, full_first, fix, full, swap, gpat, ipat, sems, work
):
    def first_core():
        swap[: 2 * B] = full_first[...]

    def second_core():
        pats = fetched(gfrom, ifrom, gpat, ipat, sems)
        work[...] = held[...]
        subtract(gpat, ipat, 3, last_t[...], dot3(couplings[3], came[...]), work, pats)
        fix_all(work, node_op, vec_op, corner, fix, swap, full)

    by_core(first_core, second_core)


def base_kernel(smoothed, fix_first, fix_second, wide_first, wide_second, ahead, came, column, out):
    def first_core():
        mats = ahead[B:]
        folded = jnp.concatenate([unpack(mats[:, 2 * B :]), unpack(mats[:, : 2 * B])], axis=0)
        partial = came[...] - dot3(folded, smoothed[:B])
        blocks = jnp.concatenate([*here(wide_first), column[...]], axis=1)
        out[...] = smoothed[...] + dot3(blocks, jnp.concatenate([fix_first[...], partial], axis=0))

    def second_core():
        out[...] = smoothed[...] + dot3(jnp.concatenate(here(wide_second), axis=1), fix_second[...])

    by_core(first_core, second_core)


def here(wide):
    return [wide[0], wide[1], wide[2], wide[NODE]]


def next_fix(came, full):
    corner = came[2 * B : 2 * B + 64]
    vec = came[:B] + dot3(unpack(corner[:, : 2 * B]), full[:B])
    node = came[B : 2 * B] + dot3(unpack(corner[:, 2 * B :]), full[B:])
    return [vec, node]


def next_term(came, full, wide):
    blocks = jnp.concatenate([wide[V_NEXT], wide[N_NEXT]], axis=1)
    return dot3(blocks, jnp.concatenate(next_fix(came, full), axis=0))


def first_end_kernel(came, full, wide, column, base, out, more, work, sem):
    def first_core():
        work[...] = base[...] + next_term(came, full, wide)
        copy = pltpu.make_async_copy(work, out, sem)
        copy.start()
        copy.wait()

    def second_core():
        more[...] = base[...] + dot3(column[...], came[: 2 * B])

    by_core(first_core, second_core)


def second_end_kernel(came, full, wide, more, _, out, work, sem):
    def second_core():
        work[...] = more[...] + next_term(came, full, wide)
        copy = pltpu.make_async_copy(work, out, sem)
        copy.start()
        copy.wait()

    pl.when(is_second())(second_core)


VMEM = pl.BlockSpec(memory_space=pltpu.VMEM)
HBM = pl.BlockSpec(memory_space=pltpu.HBM)
ANY = pl.BlockSpec(memory_space=pl.ANY)

PATTERNS = [pltpu.SMEM((2, 4), jnp.int32), pltpu.SMEM((2, 4), jnp.int32), pltpu.SemaphoreType.DMA((2,))]


def call(kernel, outs, in_specs, *args, scratch=(), units=0, out_specs=None, aliases=None):
    return pl.pallas_call(
        kernel,
        out_shape=[jax.ShapeDtypeStruct(shape, dtype) for shape, dtype in outs],
        in_specs=in_specs,
        out_specs=out_specs or [VMEM] * len(outs),
        input_output_aliases=aliases or {},
        scratch_shapes=list(scratch),
        compiler_params=pltpu.CompilerParams(vmem_limit_bytes=24 * 1024 * 1024),
        cost_estimate=pl.CostEstimate(flops=units * 50331648, bytes_accessed=units, transcendentals=0),
    )(*args)


def local(
    right_side,
    smoother,
    diagonal_blocks,
    couplings,
    grad_blocks,
    grad_pattern,
    interp_blocks,
    interp_pattern,
    node_smoother,
    vector_smoother,
    node_aggregates,
    vector_aggregates,
    node_coarse,
    vector_coarse,
):
    vectors = right_side.shape[1]
    pats = (grad_pattern.T, interp_pattern.T)

    swap, ahead, behind = chip_pairs()

    sent_ahead, sent_swap, diagonal = call(
        send_kernel,
        [((B + 64, vectors), F32), ((B, vectors), F32), ((4, B, B), F32)],
        [HBM] * 8,
        *(
            pltpu.with_memory_space_constraint(x, pltpu.HBM)
            for x in (*pats, right_side, smoother, couplings, grad_blocks, interp_blocks, diagonal_blocks)
        ),
        scratch=[
            pltpu.VMEM((2, 4), jnp.int32),
            pltpu.VMEM((2, 4), jnp.int32),
            pltpu.VMEM((B, vectors), F32),
            pltpu.VMEM((B, vectors), F32),
            pltpu.VMEM((3, B, B), F32),
            pltpu.VMEM((2, 2, B, B), F32),
            pltpu.VMEM((B, 2 * B), F32),
            pltpu.SemaphoreType.DMA((10,)),
        ],
    )
    came_ahead = crossed(sent_ahead, ahead)
    came_swap = crossed(sent_swap, swap)

    smoothed, resid, named_next = call(
        resid_kernel,
        [((4 * B, vectors), F32), ((4 * B, vectors), F32), ((2 * B, 12 * B), BF16)],
        [VMEM] * 8,
        *pats, right_side, smoother, diagonal, couplings, grad_blocks, interp_blocks,
        scratch=[pltpu.VMEM((4 * B, 2 * B), F32)],
        units=30,
    )
    (partial,) = call(
        partial_kernel,
        [((2 * B, vectors), F32)],
        [VMEM] * 3,
        came_swap, resid, named_next,
        units=0,
    )
    came_partial = crossed(partial, ahead)

    mats = (node_smoother, vector_smoother, node_aggregates, vector_aggregates, node_coarse, vector_coarse, grad_blocks, interp_blocks)
    prepared = [
        ((B, 3 * B), BF16),
        ((3 * B, 9 * B), BF16),
        ((64, vectors), F32),
        ((SLOTS, 4 * B, B), F32),
        ((4 * B, 2 * B), F32),
        ((SLOTS, B, vectors), F32),
        ((4 * B, 3 * B), BF16),
    ]
    sizes = [((4 * B, vectors), F32), ((2 * B + 64, vectors), F32), ((2 * B, vectors), F32), ((B, vectors), F32)]
    longer = ((2 * B + 72, vectors), F32)
    work = pltpu.VMEM((SLOTS, B, vectors), F32)
    node_op, vec_op, corner, wide_first, column_first, held, first_t = call(
        first_prepare_kernel,
        prepared,
        [ANY] * 2 + [VMEM] * 11 + [ANY],
        *pats, *mats, resid, came_swap, couplings, partial,
        scratch=PATTERNS,
        units=0,
    )
    fix_first, sent_back, full_first, sent_behind = call(
        first_fix_kernel,
        [sizes[0], longer, *sizes[2:]],
        [ANY] * 2 + [VMEM] * 7,
        *pats, came_ahead, first_t, held, node_op, vec_op, corner, smoothed,
        scratch=[*PATTERNS, work],
        units=0,
    )
    came_behind = crossed(sent_behind, behind)
    came_back = crossed(sent_back, behind)
    node_op, vec_op, corner, wide_second, column_second, held, last_t = call(
        second_prepare_kernel,
        prepared,
        [ANY] * 2 + [VMEM] * 11 + [ANY],
        *pats, *mats, resid, came_swap, couplings, sent_back,
        scratch=PATTERNS,
        units=100,
    )
    fix_second, full_second, sent_swap = call(
        second_fix_kernel,
        [sizes[0], sizes[2], sizes[1]],
        [ANY] * 2 + [VMEM] * 8,
        *pats, came_behind, couplings, last_t, held, node_op, vec_op, corner, full_first,
        scratch=[*PATTERNS, work],
        units=0,
    )
    came_swap = crossed(sent_swap, swap)
    (base,) = call(
        base_kernel,
        [((4 * B, vectors), F32)],
        [VMEM] * 8,
        smoothed, fix_first, fix_second, wide_first, wide_second, came_ahead, came_partial, column_first,
        units=60,
    )
    work = [pltpu.VMEM((4 * B, vectors), F32), pltpu.SemaphoreType.DMA]
    out, more = call(
        first_end_kernel,
        [((4 * B, vectors), F32)] * 2,
        [VMEM] * 5,
        came_swap, full_first, wide_first, column_second, base,
        scratch=work,
        out_specs=[ANY, VMEM],
        units=0,
    )
    (out,) = call(
        second_end_kernel,
        [((4 * B, vectors), F32)],
        [VMEM] * 4 + [ANY],
        came_back, full_second, wide_second, more, out,
        scratch=work,
        out_specs=[ANY],
        aliases={4: 0},
    )
    return out


def solution(mesh):
    in_specs = (
        P("region", None),
        P("region", None, None),
        P("region", None, None),
        P("region", None, None),
        P("region", None, None, None),
        P("region", None),
        P("region", None, None, None),
        P("region", None),
        P("region", None, None),
        P("region", None, None),
        P("region"),
        P("region"),
        P("region", None),
        P("region", None),
    )
    out_specs = P("region", None)
    return jax.shard_map(local, mesh=mesh, in_specs=in_specs, out_specs=out_specs, check_vma=False)
```

time: 45.1 us -> 38.1 us (0.84)
  starting transfers between devices: 25.5 us -> 11.5 us
  waiting for transfers between devices: 3.87 us -> 14.6 us
  Pallas kernels: 14.2 us -> 11.3 us
  local copies, waits for them, and re-layouts: 1.01 us -> 0.07 us
    ppermute x6, starting transfers between devices: 25.5 us -> 11.5 us  [crossed(): return lax.ppermute(x, 'region', pairs)]
    ppermute x6, waiting for transfers between devices: 3.87 us -> 14.6 us  [crossed(): return lax.ppermute(x, 'region', pairs)]
    pallas_call x8 -> x10, Pallas kernels: 14.2 us -> 11.3 us  [call(): pl.pallas_call(kernel, out_shape=[jax.ShapeDtypeStruct(shape, dtype) for...]
    unnamed x28 -> x26, local copies, waits for them, and re-layouts: 1.01 us -> 0.07 us
  transfers between devices with their start and end apart: 6 -> 6, of which waited for: 2 -> 4; matrix products, arithmetic and copies ran while one was open for 0% -> 0% of each run, Pallas kernels for 24% -> 25%
where the time goes in v2:
time: 38.1 us; the launch traced here: 37.8 us
  waiting for transfers between devices  14.6 us (38%)
  starting transfers between devices  11.5 us (30%)
  Pallas kernels  11.3 us (30%)
    ppermute x6, waiting for transfers between devices, crossed(): return lax.ppermute(x, 'region', pairs)  14.6 us
    ppermute x6, starting transfers between devices, crossed(): return lax.ppermute(x, 'region', pairs)  11.5 us
    pallas_call x10, Pallas kernels, call(): pl.pallas_call(kernel, out_shape=[jax.ShapeDtypeStruct(shape, dtype) for...  11.3 us
  transfers between devices with their start and end apart: 6, of which 4 were waited for; matrix products, arithmetic and copies ran while one was open for 0% of the time, Pallas kernels for 25%

profile of v2, /device:TPU:6, one launch (start us, length us, event | category | flops | bytes accessed | tf_op | source)
XLA Modules:
  0.0 37.8 jit_solution(7959227473787585394)
XLA Ops:
  0.0 0.0 copy-start
  0.0 0.0 copy-start.2
  0.0 0.0 copy-start.1
  0.0 0.0 copy-start.4
  0.0 0.0 copy-start.3
  0.0 0.0 copy-start.10
  0.0 0.0 copy-start.9
  0.0 1.9 %shard_map.136 = (f32[192,512]{1,0:T(8,128)S(1)}, f32[128,512]{1,0:T(8,128)S(1)}, f32[4,128,128]{2,1,0:T(8,128)S(1)}) custom-call(s32[2,4]{1,0:T(2,128)} %bitcast.2, s32[2,4]{1,0:T(2,128)} %bitcast.8, f32[512,512]{1,0:T(8,128)} %source.3, f32[4,128,128]{2,1,0:T(8,128)} %smoother.3, f32[4,128,128]{2,1,0:T(8,128)} %couplings.5, f32[4,2,128,128]{3,2,1,0:T(8,128)} %refs_8_.3, ...), custom_call_target="tpu_custom_call" | custom-call | tf_op jit(solution)/shard_map/pallas_call | solution.py:322
  2.0 1.3 %collective-permute-start = (f32[192,512]{1,0:T(8,128)S(1)}, f32[192,512]{1,0:T(8,128)S(1)}, u32[]{:S(2)}, u32[]{:S(2)}) collective-permute-start(f32[192,512]{1,0:T(8,128)S(1)} %get-tuple-element.34), channel_id=1, source_target_pairs={{1,2},{3,4},{5,6},{7,8},{9,10},{11,12},{13,14},{15,16},{17,18},{19... | collective-permute-start | bytes 1179656 | tf_op jit(solution)/shard_map/ppermute | solution.py:16
  3.3 4.2 %collective-permute-start.1 = (f32[128,512]{1,0:T(8,128)S(1)}, f32[128,512]{1,0:T(8,128)S(1)}, u32[]{:S(2)}, u32[]{:S(2)}) collective-permute-start(f32[128,512]{1,0:T(8,128)S(1)} %get-tuple-element.37), channel_id=1, source_target_pairs={{0,1},{1,0},{2,3},{3,2},{4,5},{5,4},{6,7},{7,6},{8,9},{9,8},{10,11... | collective-permute-start | bytes 786440 | tf_op jit(solution)/shard_map/ppermute | solution.py:16
  7.5 0.0 copy-done
  7.5 0.0 copy-done.2
  7.5 0.0 copy-done.1
  7.5 0.0 copy-done.4
  7.5 0.0 copy-done.3
  7.5 0.0 copy-done.10
  7.6 0.0 copy-done.9
  7.6 1.4 %shard_map.137 = (f32[512,512]{1,0:T(8,128)S(1)}, f32[512,512]{1,0:T(8,128)S(1)}, bf16[256,1536]{1,0:T(8,128)(2,1)S(1)}) custom-call(s32[2,4]{1,0:T(2,128)S(1)} %bitcast.3, s32[2,4]{1,0:T(2,128)S(1)} %bitcast.9, f32[512,512]{1,0:T(8,128)S(1)} %copy-done.3, f32[4,128,128]{2,1,0:T(8,128)S(1)} %copy-done.4, f32[4,128,128]{2,1,0:T(8,128)S(1)} %get-tuple-element.35.diagonal, ...), custom_call_target="tpu_custom_call" | custom-call | flops 1509949440 | bytes 30 | tf_op jit(solution)/shard_map/pallas_call | solution.py:322
  8.9 0.0 copy-start.5
  8.9 0.0 copy-start.6
  9.0 0.0 copy-start.7
  9.0 0.0 copy-start.8
  9.0 0.0 copy-start.11
  9.0 0.0 copy-start.12
  9.0 0.0 collective-permute-done.1.came.refs_11_
  9.0 1.4 %collective-permute-start.5 = (f32[256,512]{1,0:T(8,128)S(1)}, f32[256,512]{1,0:T(8,128)S(1)}, u32[]{:S(2)}, u32[]{:S(2)}) collective-permute-start(f32[256,512]{1,0:T(8,128)S(1)} %shard_map.138.refs_13_), channel_id=1, source_target_pairs={{1,2},{3,4},{5,6},{7,8},{9,10},{11,12},{13,14},{15,16},{17,18},{19... | collective-permute-start | bytes 1572872 | tf_op jit(solution)/shard_map/ppermute | solution.py:16
  10.5 0.0 copy-done.5
  10.5 0.0 copy-done.6
  10.5 0.0 copy-done.7
  10.5 0.0 copy-done.8
  10.5 0.0 copy-done.11
  10.5 0.0 copy-done.12
  10.5 3.1 %shard_map.139 = (bf16[128,384]{1,0:T(8,128)(2,1)S(1)}, bf16[384,1152]{1,0:T(8,128)(2,1)S(1)}, f32[64,512]{1,0:T(8,128)S(1)}, f32[6,512,128]{2,1,0:T(8,128)S(1)}...) custom-call(s32[2,4]{1,0:T(2,128)S(1)} %bitcast.4, s32[2,4]{1,0:T(2,128)S(1)} %bitcast.10, ...), custom_call_target="tpu_custom_call" | custom-call | tf_op jit(solution)/shard_map/pallas_call | solution.py:322
  13.7 10.3 %collective-permute-done.came.ahead = f32[192,512]{1,0:T(8,128)S(1)} collective-permute-done((f32[192,512]{1,0:T(8,128)S(1)}, f32[192,512]{1,0:T(8,128)S(1)}, u32[]{:S(2)}, u32[]{:S(2)}) %collective-permute-start) | collective-permute-done | bytes 393248 | tf_op jit(solution)/shard_map/ppermute | solution.py:16
  24.0 1.5 %shard_map.140 = (f32[512,512]{1,0:T(8,128)S(1)}, f32[328,512]{1,0:T(8,128)S(1)}, f32[256,512]{1,0:T(8,128)S(1)}, f32[128,512]{1,0:T(8,128)S(1)}) custom-call(s32[2,4]{1,0:T(2,128)S(1)} %bitcast.5, s32[2,4]{1,0:T(2,128)S(1)} %bitcast.11, f32[192,512]{1,0:T(8,128)S(1)} %collective-permute-done.came.ahead, bf16[512,384]{1,0:T(8,128)(2,1)S(1)} %get-tuple-element.39.first_t, ...), custom_call_target="tpu_custom_call" | custom-call | tf_op jit(solution)/shard_map/pallas_call | solution.py:322
  25.4 1.3 %collective-permute-start.3 = (f32[128,512]{1,0:T(8,128)S(1)}, f32[128,512]{1,0:T(8,128)S(1)}, u32[]{:S(2)}, u32[]{:S(2)}) collective-permute-start(f32[128,512]{1,0:T(8,128)S(1)} %get-tuple-element.46), channel_id=1, source_target_pairs={{2,1},{4,3},{6,5},{8,7},{10,9},{12,11},{14,13},{16,15},{18,17},{20... | collective-permute-start | bytes 786440 | tf_op jit(solution)/shard_map/ppermute | solution.py:16
  26.8 1.3 %collective-permute-start.2 = (f32[328,512]{1,0:T(8,128)S(1)}, f32[328,512]{1,0:T(8,128)S(1)}, u32[]{:S(2)}, u32[]{:S(2)}) collective-permute-start(f32[328,512]{1,0:T(8,128)S(1)} %get-tuple-element.45.refs_13_), channel_id=1, source_target_pairs={{2,1},{4,3},{6,5},{8,7},{10,9},{12,11},{14,13},{16,15},{18,17},{20... | collective-permute-start | bytes 2015240 | tf_op jit(solution)/shard_map/ppermute | solution.py:16
  28.2 2.5 %collective-permute-done.3.came = f32[128,512]{1,0:T(8,128)S(1)} collective-permute-done((f32[128,512]{1,0:T(8,128)S(1)}, f32[128,512]{1,0:T(8,128)S(1)}, u32[]{:S(2)}, u32[]{:S(2)}) %collective-permute-start.3) | collective-permute-done | bytes 262176 | tf_op jit(solution)/shard_map/ppermute | solution.py:16
  30.6 0.1 shard_map.142
  30.7 1.9 %collective-permute-start.4 = (f32[320,512]{1,0:T(8,128)S(1)}, f32[320,512]{1,0:T(8,128)S(1)}, u32[]{:S(2)}, u32[]{:S(2)}) collective-permute-start(f32[320,512]{1,0:T(8,128)S(1)} %get-tuple-element.55), channel_id=1, source_target_pairs={{0,1},{1,0},{2,3},{3,2},{4,5},{5,4},{6,7},{7,6},{8,9},{9,8},{10,11... | collective-permute-start | bytes 1966088 | tf_op jit(solution)/shard_map/ppermute | solution.py:16
  32.6 0.0 collective-permute-done.5.came
  32.6 1.5 %shard_map.143.base = f32[512,512]{1,0:T(8,128)S(1)} custom-call(f32[512,512]{1,0:T(8,128)S(1)} %get-tuple-element.44.smoothed, f32[512,512]{1,0:T(8,128)S(1)} %get-tuple-element.58.fix_first, f32[512,512]{1,0:T(8,128)S(1)} %get-tuple-element.59.fix_second, f32[6,512,128]{2,1,0:T(8,128)S(1)} %get-tuple-element.56.wide_first.wide, ...), custom_call_target="tpu_custom_call" | custom-call | flops 3019898880 | bytes 60 | tf_op jit(solution)/shard_map/pallas_call | solution.py:322
  34.2 0.5 %collective-permute-done.4.came = f32[320,512]{1,0:T(8,128)S(1)} collective-permute-done((f32[320,512]{1,0:T(8,128)S(1)}, f32[320,512]{1,0:T(8,128)S(1)}, u32[]{:S(2)}, u32[]{:S(2)}) %collective-permute-start.4) | collective-permute-done | bytes 655392 | tf_op jit(solution)/shard_map/ppermute | solution.py:16
  34.7 1.8 %shard_map.144 = (f32[512,512]{1,0:T(8,128)}, f32[512,512]{1,0:T(8,128)S(1)}) custom-call(f32[320,512]{1,0:T(8,128)S(1)} %collective-permute-done.4.came, f32[256,512]{1,0:T(8,128)S(1)} %get-tuple-element.52.full_first.full, f32[6,512,128]{2,1,0:T(8,128)S(1)} %get-tuple-element.56.wide_first.wide, f32[512,256]{1,0:T(8,128)S(1)} %get-tuple-element.57.column, ...), custom_call_target="tpu_custom_call" | custom-call | tf_op jit(solution)/shard_map/pallas_call | solution.py:322
  36.5 1.3 %collective-permute-done.2.came = f32[328,512]{1,0:T(8,128)S(1)} collective-permute-done((f32[328,512]{1,0:T(8,128)S(1)}, f32[328,512]{1,0:T(8,128)S(1)}, u32[]{:S(2)}, u32[]{:S(2)}) %collective-permute-start.2) | collective-permute-done | bytes 671776 | tf_op jit(solution)/shard_map/ppermute | solution.py:16
  (3 shorter events, 0.1 us)
Async XLA Ops:
  0.0 7.5 %copy-start = (f32[4,128,128]{2,1,0:T(8,128)S(1)}, f32[4,128,128]{2,1,0:T(8,128)}, u32[]{:S(2)}) copy-start(f32[4,128,128]{2,1,0:T(8,128)} %couplings.5) | copy-start | bytes 786436
  0.0 7.5 %copy-start.2 = (f32[4,2,128,128]{3,2,1,0:T(8,128)S(1)}, f32[4,2,128,128]{3,2,1,0:T(8,128)}, u32[]{:S(2)}) copy-start(f32[4,2,128,128]{3,2,1,0:T(8,128)} %refs_9_.3) | copy-start | bytes 1572868
  0.0 7.5 %copy-start.1 = (f32[4,2,128,128]{3,2,1,0:T(8,128)S(1)}, f32[4,2,128,128]{3,2,1,0:T(8,128)}, u32[]{:S(2)}) copy-start(f32[4,2,128,128]{3,2,1,0:T(8,128)} %refs_8_.3) | copy-start | bytes 1572868
  0.0 7.5 %copy-start.4 = (f32[4,128,128]{2,1,0:T(8,128)S(1)}, f32[4,128,128]{2,1,0:T(8,128)}, u32[]{:S(2)}) copy-start(f32[4,128,128]{2,1,0:T(8,128)} %smoother.3) | copy-start | bytes 786436
  0.0 7.5 %copy-start.3 = (f32[512,512]{1,0:T(8,128)S(1)}, f32[512,512]{1,0:T(8,128)}, u32[]{:S(2)}) copy-start(f32[512,512]{1,0:T(8,128)} %source.3) | copy-start | bytes 3145732
  0.0 7.5 %copy-start.10 = (s32[4,2]{0,1:T(2,128)S(1)}, s32[4,2]{0,1:T(2,128)}, u32[]{:S(2)}) copy-start(s32[4,2]{0,1:T(2,128)} %param.21) | copy-start | bytes 100
  0.0 7.5 %copy-start.9 = (s32[4,2]{0,1:T(2,128)S(1)}, s32[4,2]{0,1:T(2,128)}, u32[]{:S(2)}) copy-start(s32[4,2]{0,1:T(2,128)} %param.19) | copy-start | bytes 100
  2.0 22.0 %collective-permute-start = (f32[192,512]{1,0:T(8,128)S(1)}, f32[192,512]{1,0:T(8,128)S(1)}, u32[]{:S(2)}, u32[]{:S(2)}) collective-permute-start(f32[192,512]{1,0:T(8,128)S(1)} %get-tuple-element.34), channel_id=1, source_target_pairs={{1,2},{3,4},{5,6},{7,8},{9,10},{11,12},{13,14},{15,16},{17,18},{19... | collective-permute-start | bytes 1179656 | tf_op jit(solution)/shard_map/ppermute | solution.py:16
  3.3 5.8 %collective-permute-start.1 = (f32[128,512]{1,0:T(8,128)S(1)}, f32[128,512]{1,0:T(8,128)S(1)}, u32[]{:S(2)}, u32[]{:S(2)}) collective-permute-start(f32[128,512]{1,0:T(8,128)S(1)} %get-tuple-element.37), channel_id=1, source_target_pairs={{0,1},{1,0},{2,3},{3,2},{4,5},{5,4},{6,7},{7,6},{8,9},{9,8},{10,11... | collective-permute-start | bytes 786440 | tf_op jit(solution)/shard_map/ppermute | solution.py:16
  8.9 1.5 %copy-start.5 = (f32[3,128,128]{2,1,0:T(8,128)S(1)}, f32[3,128,128]{2,1,0:T(8,128)}, u32[]{:S(2)}) copy-start(f32[3,128,128]{2,1,0:T(8,128)} %refs_3_.3) | copy-start | bytes 589828
  8.9 1.5 %copy-start.6 = (f32[1,128,128]{2,1,0:T(8,128)S(1)}, f32[1,128,128]{2,1,0:T(8,128)}, u32[]{:S(2)}) copy-start(f32[1,128,128]{2,1,0:T(8,128)} %refs_2_.3) | copy-start | bytes 196612
  9.0 1.5 %copy-start.7 = (f32[128,128]{1,0:T(8,128)S(1)}, f32[128,128]{1,0:T(8,128)}, u32[]{:S(2)}) copy-start(f32[128,128]{1,0:T(8,128)} %refs_6_.3) | copy-start | bytes 196612
  9.0 1.5 %copy-start.8 = (f32[128,128]{1,0:T(8,128)S(1)}, f32[128,128]{1,0:T(8,128)}, u32[]{:S(2)}) copy-start(f32[128,128]{1,0:T(8,128)} %refs_7_.3) | copy-start | bytes 196612
  9.0 1.5 %copy-start.11 = (s32[384]{0:T(512)S(1)}, s32[384]{0:T(512)}, u32[]{:S(2)}) copy-start(s32[384]{0:T(512)} %refs_5_.3) | copy-start | bytes 4612
  9.0 1.5 %copy-start.12 = (s32[128]{0:T(128)S(1)}, s32[128]{0:T(128)}, u32[]{:S(2)}) copy-start(s32[128]{0:T(128)} %refs_4_.3) | copy-start | bytes 1540
  9.0 23.6 %collective-permute-start.5 = (f32[256,512]{1,0:T(8,128)S(1)}, f32[256,512]{1,0:T(8,128)S(1)}, u32[]{:S(2)}, u32[]{:S(2)}) collective-permute-start(f32[256,512]{1,0:T(8,128)S(1)} %shard_map.138.refs_13_), channel_id=1, source_target_pairs={{1,2},{3,4},{5,6},{7,8},{9,10},{11,12},{13,14},{15,16},{17,18},{19... | collective-permute-start | bytes 1572872 | tf_op jit(solution)/shard_map/ppermute | solution.py:16
  25.4 5.2 %collective-permute-start.3 = (f32[128,512]{1,0:T(8,128)S(1)}, f32[128,512]{1,0:T(8,128)S(1)}, u32[]{:S(2)}, u32[]{:S(2)}) collective-permute-start(f32[128,512]{1,0:T(8,128)S(1)} %get-tuple-element.46), channel_id=1, source_target_pairs={{2,1},{4,3},{6,5},{8,7},{10,9},{12,11},{14,13},{16,15},{18,17},{20... | collective-permute-start | bytes 786440 | tf_op jit(solution)/shard_map/ppermute | solution.py:16
  26.8 11.1 %collective-permute-start.2 = (f32[328,512]{1,0:T(8,128)S(1)}, f32[328,512]{1,0:T(8,128)S(1)}, u32[]{:S(2)}, u32[]{:S(2)}) collective-permute-start(f32[328,512]{1,0:T(8,128)S(1)} %get-tuple-element.45.refs_13_), channel_id=1, source_target_pairs={{2,1},{4,3},{6,5},{8,7},{10,9},{12,11},{14,13},{16,15},{18,17},{20... | collective-permute-start | bytes 2015240 | tf_op jit(solution)/shard_map/ppermute | solution.py:16
  30.7 4.0 %collective-permute-start.4 = (f32[320,512]{1,0:T(8,128)S(1)}, f32[320,512]{1,0:T(8,128)S(1)}, u32[]{:S(2)}, u32[]{:S(2)}) collective-permute-start(f32[320,512]{1,0:T(8,128)S(1)} %get-tuple-element.55), channel_id=1, source_target_pairs={{0,1},{1,0},{2,3},{3,2},{4,5},{5,4},{6,7},{7,6},{8,9},{9,8},{10,11... | collective-permute-start | bytes 1966088 | tf_op jit(solution)/shard_map/ppermute | solution.py:16

commit v3 on v2

--- a/solution.py
+++ b/solution.py
@@ -88,73 +88,72 @@
 
 
 def send_kernel(
-    gfrom, ifrom, source, smoother, couplings, grad, interp, diagonal_from, ahead, swap, diagonal,
-    gpat, ipat, last, first, mats, pairs, total, sems
+    source, smoother, couplings, diagonal_from, grad_from, interp_from, ahead, swap, diagonal, grad, interp, last, first, mats, sems
 ):
     moves = [
         (source.at[pl.ds(3 * B, B)], last),
         (smoother.at[3], mats.at[0]),
         (couplings.at[3], mats.at[1]),
-        (grad.at[3], pairs.at[0]),
-        (interp.at[3], pairs.at[1]),
-        (gfrom, gpat),
-        (ifrom, ipat),
         (source.at[pl.ds(0, B)], first),
         (smoother.at[0], mats.at[2]),
         (diagonal_from, diagonal),
+        (grad_from, grad),
+        (interp_from, interp),
     ]
     copies = [pltpu.make_async_copy(a, b, sems.at[i]) for i, (a, b) in enumerate(moves)]
     for copy in copies:
         copy.start()
-    wait_all(copies[:-1])
+    wait_all(copies[:5])
     smoothed = dot3(mats[0], last[...])
     beside = dot3(mats[2], first[...])
-    total[...] = jnp.zeros_like(total)
-    for s in range(2):
-        total[:, :B] += named(gpat, s, 3, pairs[0, s], 1)
-        total[:, B:] += named(ipat, s, 3, pairs[1, s], 3)
-    folded = dot3(total[...].T, mats[1])
-    ahead[B:, : 2 * B] = pack(folded[:B])
-    ahead[B:, 2 * B :] = pack(folded[B:])
     onward = dot3(mats[1].T, smoothed)
     ahead[:B] = onward
     swap[...] = jnp.where(is_second(), beside, onward)
-    copies[-1].wait()
-
-
-def resid_kernel(gpat, ipat, source, smoother, diagonal, couplings, grad, interp, smoothed, resid, named_next, total):
+    wait_all(copies[5:])
+
+
+def resid_kernel(gpat, ipat, source, smoother, diagonal, couplings, grad, interp, smoothed, resid, named_next, folded, total):
     for k in range(4):
         smoothed[k * B : (k + 1) * B] = dot3(smoother[k], source[k * B : (k + 1) * B])
         rows = slice(k * B, (k + 1) * B)
         total[rows, :B] = sum(named(ipat, s, k, interp[k, s], 3) for s in range(2))
         total[rows, B:] = sum(named(gpat, s, k, grad[k, s], 1) for s in range(2))
-    named_next[...] = left(total[...].T)
+    next_t = total[...].T
+    named_next[...] = left(next_t)
+    mats = dot3(next_t[:, 3 * B :], couplings[3])
+    folded[:, : 2 * B] = pack(mats[:B])
+    folded[:, 2 * B :] = pack(mats[B:])
     zero = jnp.zeros((B, B), F32)
-    rows = []
-    for k in range(4):
-        row = [zero] * 4
-        row[k] = diagonal[k]
-        if k:
-            row[k - 1] = couplings[k - 1].T
-        if k < 3:
-            row[k + 1] = couplings[k]
-        rows.append(jnp.concatenate(row, axis=1))
-    resid[...] = source[...] - mul(left(jnp.concatenate(rows, axis=0)), right(smoothed[...]))
-
-
-def partial_kernel(came, resid, named_next, partial):
+    high, low = split(smoothed[...])
+    for half in range(2):
+        rows = []
+        for k in (2 * half, 2 * half + 1):
+            row = [zero] * 3
+            row[k - half] = diagonal[k]
+            if k:
+                row[k - half - 1] = couplings[k - 1].T if k - half else row[k - half - 1]
+            if k - half < 2:
+                row[k - half + 1] = couplings[k]
+            rows.append(jnp.concatenate(row, axis=1))
+        here = slice(half * B, (half + 3) * B)
+        got = jnp.concatenate([high[here], low[here], high[here]], axis=0)
+        at = slice(2 * half * B, 2 * (half + 1) * B)
+        resid[at] = source[at] - mul(left(jnp.concatenate(rows, axis=0)), got)
+
+
+def partial_kernel(came, resid, named_next, folded, partial):
     def second_core():
         whole = jnp.concatenate([resid[:B] - came[...], resid[B:]], axis=0)
-        partial[...] = mul(named_next[...], right(whole))
+        partial[: 2 * B] = mul(named_next[...], right(whole))
+        partial[2 * B :] = folded[...]
 
     pl.when(is_second())(second_core)
 
 
-def subtract(gpat, ipat, k, blocks, x, target, pats=()):
+def subtract(blocks, x, held, work):
     terms = mul(blocks, right(x))
-    wait_all(pats)
-    for i, slot in enumerate(slots_of(gpat, ipat, k)):
-        target[slot] -= terms[i * B : (i + 1) * B]
+    for slot in range(SLOTS):
+        work[slot] = held[slot] - terms[slot * B : (slot + 1) * B]
 
 
 def operators(gpat, ipat, nsm, vsm, nagg, vagg, ncoarse, vcoarse, grad, interp, node_op, vec_op, corner, wide, column):
@@ -207,11 +206,10 @@
     grad, interp = mats[6:]
     wait_all(fetched(gfrom, ifrom, gpat, ipat, sems))
     operators(gpat, ipat, *mats, node_op, vec_op, corner, wide, column)
+    kept[...] = transposed([wide[slot, keep * B : (keep + 1) * B] for slot in range(SLOTS)])
     held[...] = jnp.zeros_like(held)
     for k in range(4):
         blocks = transposed([grad[k, 0], grad[k, 1], interp[k, 0], interp[k, 1]])
-        if k == keep:
-            kept[...] = blocks
         rows = resid[k * B : (k + 1) * B]
         if keep == 0 and k == 3:
             rows = rows - dot3(couplings[3], came[...])
@@ -231,38 +229,34 @@
 
 
 def first_fix_kernel(
-    gfrom, ifrom, came, first_t, held, node_op, vec_op, corner, smoothed, fix, back, full, behind, gpat, ipat, sems, work
+    came, first_t, held, node_op, vec_op, corner, smoothed, fix, back, full, behind, work
 ):
     def first_core():
-        pats = fetched(gfrom, ifrom, gpat, ipat, sems)
         behind[...] = smoothed[:B]
-        work[...] = held[...]
-        subtract(gpat, ipat, 0, first_t[...], came[:B], work, pats)
+        subtract(first_t[...], came[:B], held, work)
         fix_all(work, node_op, vec_op, corner, fix, back, full)
 
     pl.when(jnp.logical_not(is_second()))(first_core)
 
 
 def second_fix_kernel(
-    gfrom, ifrom, came, couplings, last_t, held, node_op, vec_op, corner, full_first, fix, full, swap, gpat, ipat, sems, work
+    came, couplings, last_t, held, node_op, vec_op, corner, full_first, fix, full, swap, work
 ):
     def first_core():
         swap[: 2 * B] = full_first[...]
 
     def second_core():
-        pats = fetched(gfrom, ifrom, gpat, ipat, sems)
-        work[...] = held[...]
-        subtract(gpat, ipat, 3, last_t[...], dot3(couplings[3], came[...]), work, pats)
+        subtract(last_t[...], dot3(couplings[3], came[...]), held, work)
         fix_all(work, node_op, vec_op, corner, fix, swap, full)
 
     by_core(first_core, second_core)
 
 
-def base_kernel(smoothed, fix_first, fix_second, wide_first, wide_second, ahead, came, column, out):
+def base_kernel(smoothed, fix_first, fix_second, wide_first, wide_second, came, column, out):
     def first_core():
-        mats = ahead[B:]
-        folded = jnp.concatenate([unpack(mats[:, 2 * B :]), unpack(mats[:, : 2 * B])], axis=0)
-        partial = came[...] - dot3(folded, smoothed[:B])
+        mats = came[2 * B :]
+        folded = jnp.concatenate([unpack(mats[:, : 2 * B]), unpack(mats[:, 2 * B :])], axis=0)
+        partial = came[: 2 * B] - dot3(folded, smoothed[:B])
         blocks = jnp.concatenate([*here(wide_first), column[...]], axis=1)
         out[...] = smoothed[...] + dot3(blocks, jnp.concatenate([fix_first[...], partial], axis=0))
 
@@ -352,41 +346,35 @@
 
     swap, ahead, behind = chip_pairs()
 
-    sent_ahead, sent_swap, diagonal = call(
+    fetched_here = (diagonal_blocks, grad_blocks, interp_blocks)
+    sent_ahead, sent_swap, diagonal, grad_blocks, interp_blocks = call(
         send_kernel,
-        [((B + 64, vectors), F32), ((B, vectors), F32), ((4, B, B), F32)],
-        [HBM] * 8,
-        *(
-            pltpu.with_memory_space_constraint(x, pltpu.HBM)
-            for x in (*pats, right_side, smoother, couplings, grad_blocks, interp_blocks, diagonal_blocks)
-        ),
+        [((B + 8, vectors), F32), ((B, vectors), F32), *((x.shape, F32) for x in fetched_here)],
+        [HBM] * 6,
+        *(pltpu.with_memory_space_constraint(x, pltpu.HBM) for x in (right_side, smoother, couplings, *fetched_here)),
         scratch=[
-            pltpu.VMEM((2, 4), jnp.int32),
-            pltpu.VMEM((2, 4), jnp.int32),
             pltpu.VMEM((B, vectors), F32),
             pltpu.VMEM((B, vectors), F32),
             pltpu.VMEM((3, B, B), F32),
-            pltpu.VMEM((2, 2, B, B), F32),
-            pltpu.VMEM((B, 2 * B), F32),
-            pltpu.SemaphoreType.DMA((10,)),
+            pltpu.SemaphoreType.DMA((8,)),
         ],
     )
     came_ahead = crossed(sent_ahead, ahead)
     came_swap = crossed(sent_swap, swap)
 
-    smoothed, resid, named_next = call(
+    smoothed, resid, named_next, folded = call(
         resid_kernel,
-        [((4 * B, vectors), F32), ((4 * B, vectors), F32), ((2 * B, 12 * B), BF16)],
+        [((4 * B, vectors), F32), ((4 * B, vectors), F32), ((2 * B, 12 * B), BF16), ((64, vectors), F32)],
         [VMEM] * 8,
         *pats, right_side, smoother, diagonal, couplings, grad_blocks, interp_blocks,
         scratch=[pltpu.VMEM((4 * B, 2 * B), F32)],
-        units=30,
+        units=0,
     )
     (partial,) = call(
         partial_kernel,
-        [((2 * B, vectors), F32)],
-        [VMEM] * 3,
-        came_swap, resid, named_next,
+        [((2 * B + 64, vectors), F32)],
+        [VMEM] * 4,
+        came_swap, resid, named_next, folded,
         units=0,
     )
     came_partial = crossed(partial, ahead)
@@ -399,7 +387,7 @@
         ((SLOTS, 4 * B, B), F32),
         ((4 * B, 2 * B), F32),
         ((SLOTS, B, vectors), F32),
-        ((4 * B, 3 * B), BF16),
+        ((SLOTS * B, 3 * B), BF16),
     ]
     sizes = [((4 * B, vectors), F32), ((2 * B + 64, vectors), F32), ((2 * B, vectors), F32), ((B, vectors), F32)]
     longer = ((2 * B + 72, vectors), F32)
@@ -415,9 +403,9 @@
     fix_first, sent_back, full_first, sent_behind = call(
         first_fix_kernel,
         [sizes[0], longer, *sizes[2:]],
-        [ANY] * 2 + [VMEM] * 7,
-        *pats, came_ahead, first_t, held, node_op, vec_op, corner, smoothed,
-        scratch=[*PATTERNS, work],
+        [VMEM] * 7,
+        came_ahead, first_t, held, node_op, vec_op, corner, smoothed,
+        scratch=[work],
         units=0,
     )
     came_behind = crossed(sent_behind, behind)
@@ -433,17 +421,17 @@
     fix_second, full_second, sent_swap = call(
         second_fix_kernel,
         [sizes[0], sizes[2], sizes[1]],
-        [ANY] * 2 + [VMEM] * 8,
-        *pats, came_behind, couplings, last_t, held, node_op, vec_op, corner, full_first,
-        scratch=[*PATTERNS, work],
+        [VMEM] * 8,
+        came_behind, couplings, last_t, held, node_op, vec_op, corner, full_first,
+        scratch=[work],
         units=0,
     )
     came_swap = crossed(sent_swap, swap)
     (base,) = call(
         base_kernel,
         [((4 * B, vectors), F32)],
-        [VMEM] * 8,
-        smoothed, fix_first, fix_second, wide_first, wide_second, came_ahead, came_partial, column_first,
+        [VMEM] * 7,
+        smoothed, fix_first, fix_second, wide_first, wide_second, came_partial, column_first,
         units=60,
     )
     work = [pltpu.VMEM((4 * B, vectors), F32), pltpu.SemaphoreType.DMA]

time: 38.1 us -> 37.7 us (0.990)
  starting transfers between devices: 11.5 us -> 12.9 us
  waiting for transfers between devices: 14.6 us -> 13.5 us
  Pallas kernels: 11.3 us -> 10.8 us
    ppermute x6, starting transfers between devices: 11.5 us -> 12.9 us  [crossed(): return lax.ppermute(x, 'region', pairs)]
    ppermute x6, waiting for transfers between devices: 14.6 us -> 13.5 us  [crossed(): return lax.ppermute(x, 'region', pairs)]
    pallas_call x10, Pallas kernels: 11.3 us -> 10.8 us  [call(): pl.pallas_call(kernel, out_shape=[jax.ShapeDtypeStruct(shape, dtype) for...]
  transfers between devices with their start and end apart: 6 -> 6, of which waited for: 4 -> 5; matrix products, arithmetic and copies ran while one was open for 0% -> 0% of each run, Pallas kernels for 25% -> 24%
where the time goes in v3:
time: 37.7 us; the launch traced here: 37.5 us
  waiting for transfers between devices  13.5 us (36%)
  starting transfers between devices  12.9 us (34%)
  Pallas kernels  10.8 us (29%)
    ppermute x6, waiting for transfers between devices, crossed(): return lax.ppermute(x, 'region', pairs)  13.5 us
    ppermute x6, starting transfers between devices, crossed(): return lax.ppermute(x, 'region', pairs)  12.9 us
    pallas_call x10, Pallas kernels, call(): pl.pallas_call(kernel, out_shape=[jax.ShapeDtypeStruct(shape, dtype) for...  10.8 us
  transfers between devices with their start and end apart: 6, of which 5 were waited for; matrix products, arithmetic and copies ran while one was open for 0% of the time, Pallas kernels for 24%

profile of v3, /device:TPU:6, one launch (start us, length us, event | category | flops | bytes accessed | tf_op | source)
XLA Modules:
  0.0 37.5 jit_solution(17709243268046852304)
XLA Ops:
  0.0 0.0 copy-start.1
  0.0 0.0 copy-start.2
  0.0 0.0 copy-start
  0.0 0.0 copy-start.7
  0.0 0.0 copy-start.8
  0.0 1.7 %shard_map.136 = (f32[136,512]{1,0:T(8,128)S(1)}, f32[128,512]{1,0:T(8,128)S(1)}, f32[4,128,128]{2,1,0:T(8,128)S(1)}, f32[4,2,128,128]{3,2,1,0:T(8,128)S(1)}, f32[4,2,128,128]{3,2,1,0:T(8,128)S(1)}) custom-call(f32[512,512]{1,0:T(8,128)} %source.3, f32[4,128,128]{2,1,0:T(8,128)} %smoother.3, f32[4,128,128]{2,1,0:T(8,128)} %couplings.5, ...), custom_call_target="tpu_custom_call" | custom-call | tf_op jit(solution)/shard_map/pallas_call | solution.py:316
  1.8 1.3 %collective-permute-start = (f32[136,512]{1,0:T(8,128)S(1)}, f32[136,512]{1,0:T(8,128)S(1)}, u32[]{:S(2)}, u32[]{:S(2)}) collective-permute-start(f32[136,512]{1,0:T(8,128)S(1)} %get-tuple-element.37), channel_id=1, source_target_pairs={{1,2},{3,4},{5,6},{7,8},{9,10},{11,12},{13,14},{15,16},{17,18},{19... | collective-permute-start | bytes 835592 | tf_op jit(solution)/shard_map/ppermute | solution.py:16
  3.1 4.2 %collective-permute-start.1 = (f32[128,512]{1,0:T(8,128)S(1)}, f32[128,512]{1,0:T(8,128)S(1)}, u32[]{:S(2)}, u32[]{:S(2)}) collective-permute-start(f32[128,512]{1,0:T(8,128)S(1)} %get-tuple-element.42), channel_id=1, source_target_pairs={{0,1},{1,0},{2,3},{3,2},{4,5},{5,4},{6,7},{7,6},{8,9},{9,8},{10,11... | collective-permute-start | bytes 786440 | tf_op jit(solution)/shard_map/ppermute | solution.py:16
  7.3 0.0 copy-done.1
  7.3 0.0 copy-done.2
  7.3 0.0 copy-done
  7.3 0.0 copy-done.7
  7.4 0.0 copy-done.8
  7.4 1.3 %shard_map.137 = (f32[512,512]{1,0:T(8,128)S(1)}, f32[512,512]{1,0:T(8,128)S(1)}, bf16[256,1536]{1,0:T(8,128)(2,1)S(1)}, f32[64,512]{1,0:T(8,128)S(1)}) custom-call(s32[2,4]{1,0:T(2,128)S(1)} %bitcast.2, s32[2,4]{1,0:T(2,128)S(1)} %bitcast.5, f32[512,512]{1,0:T(8,128)S(1)} %copy-done.1, f32[4,128,128]{2,1,0:T(8,128)S(1)} %copy-done.2, ...), custom_call_target="tpu_custom_call" | custom-call | tf_op jit(solution)/shard_map/pallas_call | solution.py:316
  8.7 0.0 copy-start.3
  8.7 0.0 copy-start.4
  8.7 0.0 copy-start.5
  8.7 0.0 copy-start.6
  8.8 0.0 copy-start.9
  8.8 0.0 copy-start.10
  8.8 0.0 collective-permute-done.1.came.refs_11_
  8.8 1.4 %collective-permute-start.5 = (f32[320,512]{1,0:T(8,128)S(1)}, f32[320,512]{1,0:T(8,128)S(1)}, u32[]{:S(2)}, u32[]{:S(2)}) collective-permute-start(f32[320,512]{1,0:T(8,128)S(1)} %shard_map.138.refs_13_), channel_id=1, source_target_pairs={{1,2},{3,4},{5,6},{7,8},{9,10},{11,12},{13,14},{15,16},{17,18},{19... | collective-permute-start | bytes 1966088 | tf_op jit(solution)/shard_map/ppermute | solution.py:16
  10.2 0.0 copy-done.3
  10.3 0.0 copy-done.4
  10.3 0.0 copy-done.5
  10.3 0.0 copy-done.6
  10.3 0.0 copy-done.9
  10.3 0.0 copy-done.10
  10.3 3.1 %shard_map.139 = (bf16[128,384]{1,0:T(8,128)(2,1)S(1)}, bf16[384,1152]{1,0:T(8,128)(2,1)S(1)}, f32[64,512]{1,0:T(8,128)S(1)}, f32[6,512,128]{2,1,0:T(8,128)S(1)}...) custom-call(s32[2,4]{1,0:T(2,128)S(1)} %bitcast.3, s32[2,4]{1,0:T(2,128)S(1)} %bitcast.6, ...), custom_call_target="tpu_custom_call" | custom-call | tf_op jit(solution)/shard_map/pallas_call | solution.py:316
  13.4 9.2 %collective-permute-done.came = f32[136,512]{1,0:T(8,128)S(1)} collective-permute-done((f32[136,512]{1,0:T(8,128)S(1)}, f32[136,512]{1,0:T(8,128)S(1)}, u32[]{:S(2)}, u32[]{:S(2)}) %collective-permute-start) | collective-permute-done | bytes 278560 | tf_op jit(solution)/shard_map/ppermute | solution.py:16
  22.6 1.2 %shard_map.140 = (f32[512,512]{1,0:T(8,128)S(1)}, f32[328,512]{1,0:T(8,128)S(1)}, f32[256,512]{1,0:T(8,128)S(1)}, f32[128,512]{1,0:T(8,128)S(1)}) custom-call(f32[136,512]{1,0:T(8,128)S(1)} %collective-permute-done.came, bf16[768,384]{1,0:T(8,128)(2,1)S(1)} %get-tuple-element.45.first_t, f32[6,128,512]{2,1,0:T(8,128)S(1)} %get-tuple-element.46.held, ...), custom_call_target="tpu_custom_call" | custom-call | tf_op jit(solution)/shard_map/pallas_call | solution.py:316
  23.8 2.7 %collective-permute-start.3 = (f32[128,512]{1,0:T(8,128)S(1)}, f32[128,512]{1,0:T(8,128)S(1)}, u32[]{:S(2)}, u32[]{:S(2)}) collective-permute-start(f32[128,512]{1,0:T(8,128)S(1)} %get-tuple-element.52), channel_id=1, source_target_pairs={{2,1},{4,3},{6,5},{8,7},{10,9},{12,11},{14,13},{16,15},{18,17},{20... | collective-permute-start | bytes 786440 | tf_op jit(solution)/shard_map/ppermute | solution.py:16
  26.5 1.3 %collective-permute-start.2 = (f32[328,512]{1,0:T(8,128)S(1)}, f32[328,512]{1,0:T(8,128)S(1)}, u32[]{:S(2)}, u32[]{:S(2)}) collective-permute-start(f32[328,512]{1,0:T(8,128)S(1)} %get-tuple-element.51.refs_13_), channel_id=1, source_target_pairs={{2,1},{4,3},{6,5},{8,7},{10,9},{12,11},{14,13},{16,15},{18,17},{20... | collective-permute-start | bytes 2015240 | tf_op jit(solution)/shard_map/ppermute | solution.py:16
  27.9 2.5 %collective-permute-done.3.came = f32[128,512]{1,0:T(8,128)S(1)} collective-permute-done((f32[128,512]{1,0:T(8,128)S(1)}, f32[128,512]{1,0:T(8,128)S(1)}, u32[]{:S(2)}, u32[]{:S(2)}) %collective-permute-start.3) | collective-permute-done | bytes 262176 | tf_op jit(solution)/shard_map/ppermute | solution.py:16
  30.4 1.9 %collective-permute-start.4 = (f32[320,512]{1,0:T(8,128)S(1)}, f32[320,512]{1,0:T(8,128)S(1)}, u32[]{:S(2)}, u32[]{:S(2)}) collective-permute-start(f32[320,512]{1,0:T(8,128)S(1)} %get-tuple-element.61), channel_id=1, source_target_pairs={{0,1},{1,0},{2,3},{3,2},{4,5},{5,4},{6,7},{7,6},{8,9},{9,8},{10,11... | collective-permute-start | bytes 1966088 | tf_op jit(solution)/shard_map/ppermute | solution.py:16
  32.3 0.3 collective-permute-done.5.came
  32.6 1.5 %shard_map.143.base = f32[512,512]{1,0:T(8,128)S(1)} custom-call(f32[512,512]{1,0:T(8,128)S(1)} %get-tuple-element.50.smoothed, f32[512,512]{1,0:T(8,128)S(1)} %get-tuple-element.64.fix_first, f32[512,512]{1,0:T(8,128)S(1)} %get-tuple-element.65.fix_second, f32[6,512,128]{2,1,0:T(8,128)S(1)} %get-tuple-element.62.wide_first.wide, ...), custom_call_target="tpu_custom_call" | custom-call | flops 3019898880 | bytes 60 | tf_op jit(solution)/shard_map/pallas_call | solution.py:316
  34.1 0.2 collective-permute-done.4.came
  34.4 1.8 %shard_map.144 = (f32[512,512]{1,0:T(8,128)}, f32[512,512]{1,0:T(8,128)S(1)}) custom-call(f32[320,512]{1,0:T(8,128)S(1)} %collective-permute-done.4.came, f32[256,512]{1,0:T(8,128)S(1)} %get-tuple-element.58.full_first.full, f32[6,512,128]{2,1,0:T(8,128)S(1)} %get-tuple-element.62.wide_first.wide, f32[512,256]{1,0:T(8,128)S(1)} %get-tuple-element.63.column, ...), custom_call_target="tpu_custom_call" | custom-call | tf_op jit(solution)/shard_map/pallas_call | solution.py:316
  36.2 1.3 %collective-permute-done.2.came = f32[328,512]{1,0:T(8,128)S(1)} collective-permute-done((f32[328,512]{1,0:T(8,128)S(1)}, f32[328,512]{1,0:T(8,128)S(1)}, u32[]{:S(2)}, u32[]{:S(2)}) %collective-permute-start.2) | collective-permute-done | bytes 671776 | tf_op jit(solution)/shard_map/ppermute | solution.py:16
  (4 shorter events, 0.1 us)
Async XLA Ops:
  0.0 7.3 %copy-start.1 = (f32[512,512]{1,0:T(8,128)S(1)}, f32[512,512]{1,0:T(8,128)}, u32[]{:S(2)}) copy-start(f32[512,512]{1,0:T(8,128)} %source.3) | copy-start | bytes 3145732
  0.0 7.3 %copy-start.2 = (f32[4,128,128]{2,1,0:T(8,128)S(1)}, f32[4,128,128]{2,1,0:T(8,128)}, u32[]{:S(2)}) copy-start(f32[4,128,128]{2,1,0:T(8,128)} %smoother.3) | copy-start | bytes 786436
  0.0 7.3 %copy-start = (f32[4,128,128]{2,1,0:T(8,128)S(1)}, f32[4,128,128]{2,1,0:T(8,128)}, u32[]{:S(2)}) copy-start(f32[4,128,128]{2,1,0:T(8,128)} %couplings.5) | copy-start | bytes 786436
  0.0 7.3 %copy-start.7 = (s32[4,2]{0,1:T(2,128)S(1)}, s32[4,2]{0,1:T(2,128)}, u32[]{:S(2)}) copy-start(s32[4,2]{0,1:T(2,128)} %param.19) | copy-start | bytes 100
  0.0 7.3 %copy-start.8 = (s32[4,2]{0,1:T(2,128)S(1)}, s32[4,2]{0,1:T(2,128)}, u32[]{:S(2)}) copy-start(s32[4,2]{0,1:T(2,128)} %param.21) | copy-start | bytes 100
  1.8 20.8 %collective-permute-start = (f32[136,512]{1,0:T(8,128)S(1)}, f32[136,512]{1,0:T(8,128)S(1)}, u32[]{:S(2)}, u32[]{:S(2)}) collective-permute-start(f32[136,512]{1,0:T(8,128)S(1)} %get-tuple-element.37), channel_id=1, source_target_pairs={{1,2},{3,4},{5,6},{7,8},{9,10},{11,12},{13,14},{15,16},{17,18},{19... | collective-permute-start | bytes 835592 | tf_op jit(solution)/shard_map/ppermute | solution.py:16
  3.1 5.7 %collective-permute-start.1 = (f32[128,512]{1,0:T(8,128)S(1)}, f32[128,512]{1,0:T(8,128)S(1)}, u32[]{:S(2)}, u32[]{:S(2)}) collective-permute-start(f32[128,512]{1,0:T(8,128)S(1)} %get-tuple-element.42), channel_id=1, source_target_pairs={{0,1},{1,0},{2,3},{3,2},{4,5},{5,4},{6,7},{7,6},{8,9},{9,8},{10,11... | collective-permute-start | bytes 786440 | tf_op jit(solution)/shard_map/ppermute | solution.py:16
  8.7 1.5 %copy-start.3 = (f32[3,128,128]{2,1,0:T(8,128)S(1)}, f32[3,128,128]{2,1,0:T(8,128)}, u32[]{:S(2)}) copy-start(f32[3,128,128]{2,1,0:T(8,128)} %refs_3_.3) | copy-start | bytes 589828
  8.7 1.5 %copy-start.4 = (f32[1,128,128]{2,1,0:T(8,128)S(1)}, f32[1,128,128]{2,1,0:T(8,128)}, u32[]{:S(2)}) copy-start(f32[1,128,128]{2,1,0:T(8,128)} %refs_2_.3) | copy-start | bytes 196612
  8.7 1.5 %copy-start.5 = (f32[128,128]{1,0:T(8,128)S(1)}, f32[128,128]{1,0:T(8,128)}, u32[]{:S(2)}) copy-start(f32[128,128]{1,0:T(8,128)} %refs_6_.3) | copy-start | bytes 196612
  8.7 1.5 %copy-start.6 = (f32[128,128]{1,0:T(8,128)S(1)}, f32[128,128]{1,0:T(8,128)}, u32[]{:S(2)}) copy-start(f32[128,128]{1,0:T(8,128)} %refs_7_.3) | copy-start | bytes 196612
  8.8 1.5 %copy-start.9 = (s32[384]{0:T(512)S(1)}, s32[384]{0:T(512)}, u32[]{:S(2)}) copy-start(s32[384]{0:T(512)} %refs_5_.3) | copy-start | bytes 4612
  8.8 1.5 %copy-start.10 = (s32[128]{0:T(128)S(1)}, s32[128]{0:T(128)}, u32[]{:S(2)}) copy-start(s32[128]{0:T(128)} %refs_4_.3) | copy-start | bytes 1540
  8.8 23.8 %collective-permute-start.5 = (f32[320,512]{1,0:T(8,128)S(1)}, f32[320,512]{1,0:T(8,128)S(1)}, u32[]{:S(2)}, u32[]{:S(2)}) collective-permute-start(f32[320,512]{1,0:T(8,128)S(1)} %shard_map.138.refs_13_), channel_id=1, source_target_pairs={{1,2},{3,4},{5,6},{7,8},{9,10},{11,12},{13,14},{15,16},{17,18},{19... | collective-permute-start | bytes 1966088 | tf_op jit(solution)/shard_map/ppermute | solution.py:16
  23.8 6.6 %collective-permute-start.3 = (f32[128,512]{1,0:T(8,128)S(1)}, f32[128,512]{1,0:T(8,128)S(1)}, u32[]{:S(2)}, u32[]{:S(2)}) collective-permute-start(f32[128,512]{1,0:T(8,128)S(1)} %get-tuple-element.52), channel_id=1, source_target_pairs={{2,1},{4,3},{6,5},{8,7},{10,9},{12,11},{14,13},{16,15},{18,17},{20... | collective-permute-start | bytes 786440 | tf_op jit(solution)/shard_map/ppermute | solution.py:16
  26.5 11.1 %collective-permute-start.2 = (f32[328,512]{1,0:T(8,128)S(1)}, f32[328,512]{1,0:T(8,128)S(1)}, u32[]{:S(2)}, u32[]{:S(2)}) collective-permute-start(f32[328,512]{1,0:T(8,128)S(1)} %get-tuple-element.51.refs_13_), channel_id=1, source_target_pairs={{2,1},{4,3},{6,5},{8,7},{10,9},{12,11},{14,13},{16,15},{18,17},{20... | collective-permute-start | bytes 2015240 | tf_op jit(solution)/shard_map/ppermute | solution.py:16
  30.4 4.0 %collective-permute-start.4 = (f32[320,512]{1,0:T(8,128)S(1)}, f32[320,512]{1,0:T(8,128)S(1)}, u32[]{:S(2)}, u32[]{:S(2)}) collective-permute-start(f32[320,512]{1,0:T(8,128)S(1)} %get-tuple-element.61), channel_id=1, source_target_pairs={{0,1},{1,0},{2,3},{3,2},{4,5},{5,4},{6,7},{7,6},{8,9},{9,8},{10,11... | collective-permute-start | bytes 1966088 | tf_op jit(solution)/shard_map/ppermute | solution.py:16

commit v4 on v3

--- a/solution.py
+++ b/solution.py
@@ -112,14 +112,14 @@
     wait_all(copies[5:])
 
 
-def resid_kernel(gpat, ipat, source, smoother, diagonal, couplings, grad, interp, smoothed, resid, named_next, folded, total):
+def resid_kernel(gpat, ipat, source, smoother, diagonal, couplings, grad, interp, smoothed, resid, first_next, local_next, folded, total):
     for k in range(4):
         smoothed[k * B : (k + 1) * B] = dot3(smoother[k], source[k * B : (k + 1) * B])
         rows = slice(k * B, (k + 1) * B)
         total[rows, :B] = sum(named(ipat, s, k, interp[k, s], 3) for s in range(2))
         total[rows, B:] = sum(named(gpat, s, k, grad[k, s], 1) for s in range(2))
     next_t = total[...].T
-    named_next[...] = left(next_t)
+    first_next[...] = left(next_t[:, :B])
     mats = dot3(next_t[:, 3 * B :], couplings[3])
     folded[:, : 2 * B] = pack(mats[:B])
     folded[:, 2 * B :] = pack(mats[B:])
@@ -139,12 +139,12 @@
         got = jnp.concatenate([high[here], low[here], high[here]], axis=0)
         at = slice(2 * half * B, 2 * (half + 1) * B)
         resid[at] = source[at] - mul(left(jnp.concatenate(rows, axis=0)), got)
-
-
-def partial_kernel(came, resid, named_next, folded, partial):
+    local_next[...] = mul(left(next_t), right(resid[...]))
+
+
+def partial_kernel(came, first_next, local_next, folded, partial):
     def second_core():
-        whole = jnp.concatenate([resid[:B] - came[...], resid[B:]], axis=0)
-        partial[: 2 * B] = mul(named_next[...], right(whole))
+        partial[: 2 * B] = local_next[...] - mul(first_next[...], right(came[...]))
         partial[2 * B :] = folded[...]
 
     pl.when(is_second())(second_core)
@@ -362,9 +362,9 @@
     came_ahead = crossed(sent_ahead, ahead)
     came_swap = crossed(sent_swap, swap)
 
-    smoothed, resid, named_next, folded = call(
+    smoothed, resid, first_next, local_next, folded = call(
         resid_kernel,
-        [((4 * B, vectors), F32), ((4 * B, vectors), F32), ((2 * B, 12 * B), BF16), ((64, vectors), F32)],
+        [((4 * B, vectors), F32), ((4 * B, vectors), F32), ((2 * B, 3 * B), BF16), ((2 * B, vectors), F32), ((64, vectors), F32)],
         [VMEM] * 8,
         *pats, right_side, smoother, diagonal, couplings, grad_blocks, interp_blocks,
         scratch=[pltpu.VMEM((4 * B, 2 * B), F32)],
@@ -374,7 +374,7 @@
         partial_kernel,
         [((2 * B + 64, vectors), F32)],
         [VMEM] * 4,
-        came_swap, resid, named_next, folded,
+        came_swap, first_next, local_next, folded,
         units=0,
     )
     came_partial = crossed(partial, ahead)

time: 37.7 us -> 37.9 us (level)
  Pallas kernels: 10.8 us -> 11.3 us
  waiting for transfers between devices: 13.5 us -> 13 us
    pallas_call x10, Pallas kernels: 10.8 us -> 11.3 us  [call(): pl.pallas_call(kernel, out_shape=[jax.ShapeDtypeStruct(shape, dtype) for...]
    ppermute x6, waiting for transfers between devices: 13.5 us -> 13 us  [crossed(): return lax.ppermute(x, 'region', pairs)]
  transfers between devices with their start and end apart: 6 -> 6, of which waited for: 5 -> 5; matrix products, arithmetic and copies ran while one was open for 0% -> 0% of each run, Pallas kernels for 24% -> 25%
where the time goes in v4:
time: 37.9 us; the launch traced here: 37.7 us
  starting transfers between devices  13 us (34%)
  waiting for transfers between devices  13 us (34%)
  Pallas kernels  11.3 us (30%)
    ppermute x6, starting transfers between devices, crossed(): return lax.ppermute(x, 'region', pairs)  13 us
    ppermute x6, waiting for transfers between devices, crossed(): return lax.ppermute(x, 'region', pairs)  13 us
    pallas_call x10, Pallas kernels, call(): pl.pallas_call(kernel, out_shape=[jax.ShapeDtypeStruct(shape, dtype) for...  11.3 us
  transfers between devices with their start and end apart: 6, of which 5 were waited for; matrix products, arithmetic and copies ran while one was open for 0% of the time, Pallas kernels for 25%

profile of v4, /device:TPU:6, one launch (start us, length us, event | category | flops | bytes accessed | tf_op | source)
XLA Modules:
  0.0 37.7 jit_solution(13110416391483982685)
XLA Ops:
  0.0 0.0 copy-start.1
  0.0 0.0 copy-start.2
  0.0 0.0 copy-start
  0.0 0.0 copy-start.7
  0.0 0.0 copy-start.8
  0.0 1.7 %shard_map.136 = (f32[136,512]{1,0:T(8,128)S(1)}, f32[128,512]{1,0:T(8,128)S(1)}, f32[4,128,128]{2,1,0:T(8,128)S(1)}, f32[4,2,128,128]{3,2,1,0:T(8,128)S(1)}, f32[4,2,128,128]{3,2,1,0:T(8,128)S(1)}) custom-call(f32[512,512]{1,0:T(8,128)} %source.3, f32[4,128,128]{2,1,0:T(8,128)} %smoother.3, f32[4,128,128]{2,1,0:T(8,128)} %couplings.5, ...), custom_call_target="tpu_custom_call" | custom-call | tf_op jit(solution)/shard_map/pallas_call | solution.py:316
  1.8 1.3 %collective-permute-start = (f32[136,512]{1,0:T(8,128)S(1)}, f32[136,512]{1,0:T(8,128)S(1)}, u32[]{:S(2)}, u32[]{:S(2)}) collective-permute-start(f32[136,512]{1,0:T(8,128)S(1)} %get-tuple-element.38), channel_id=1, source_target_pairs={{1,2},{3,4},{5,6},{7,8},{9,10},{11,12},{13,14},{15,16},{17,18},{19... | collective-permute-start | bytes 835592 | tf_op jit(solution)/shard_map/ppermute | solution.py:16
  3.1 4.2 %collective-permute-start.1 = (f32[128,512]{1,0:T(8,128)S(1)}, f32[128,512]{1,0:T(8,128)S(1)}, u32[]{:S(2)}, u32[]{:S(2)}) collective-permute-start(f32[128,512]{1,0:T(8,128)S(1)} %get-tuple-element.43), channel_id=1, source_target_pairs={{0,1},{1,0},{2,3},{3,2},{4,5},{5,4},{6,7},{7,6},{8,9},{9,8},{10,11... | collective-permute-start | bytes 786440 | tf_op jit(solution)/shard_map/ppermute | solution.py:16
  7.3 0.0 copy-done.1
  7.3 0.0 copy-done.2
  7.3 0.0 copy-done
  7.3 0.0 copy-done.7
  7.4 0.0 copy-done.8
  7.4 1.8 %shard_map.137 = (f32[512,512]{1,0:T(8,128)S(1)}, f32[512,512]{1,0:T(8,128)S(1)}, bf16[256,384]{1,0:T(8,128)(2,1)S(1)}, f32[256,512]{1,0:T(8,128)S(1)}, f32[64,512]{1,0:T(8,128)S(1)}) custom-call(s32[2,4]{1,0:T(2,128)S(1)} %bitcast.2, s32[2,4]{1,0:T(2,128)S(1)} %bitcast.5, f32[512,512]{1,0:T(8,128)S(1)} %copy-done.1, f32[4,128,128]{2,1,0:T(8,128)S(1)} %copy-done.2, ...), custom_call_target="tpu_custom_call" | custom-call | tf_op jit(solution)/shard_map/pallas_call | solution.py:316
  9.1 0.0 copy-start.3
  9.2 0.0 copy-start.4
  9.2 0.0 copy-start.5
  9.2 0.0 copy-start.6
  9.2 0.0 copy-start.9
  9.2 0.0 copy-start.10
  9.2 0.0 collective-permute-done.1.came.refs_11_
  9.3 1.4 %collective-permute-start.5 = (f32[320,512]{1,0:T(8,128)S(1)}, f32[320,512]{1,0:T(8,128)S(1)}, u32[]{:S(2)}, u32[]{:S(2)}) collective-permute-start(f32[320,512]{1,0:T(8,128)S(1)} %shard_map.138.refs_13_), channel_id=1, source_target_pairs={{1,2},{3,4},{5,6},{7,8},{9,10},{11,12},{13,14},{15,16},{17,18},{19... | collective-permute-start | bytes 1966088 | tf_op jit(solution)/shard_map/ppermute | solution.py:16
  10.7 0.0 copy-done.3
  10.7 0.0 copy-done.4
  10.7 0.0 copy-done.5
  10.7 0.0 copy-done.6
  10.7 0.0 copy-done.9
  10.7 0.0 copy-done.10
  10.7 3.1 %shard_map.139 = (bf16[128,384]{1,0:T(8,128)(2,1)S(1)}, bf16[384,1152]{1,0:T(8,128)(2,1)S(1)}, f32[64,512]{1,0:T(8,128)S(1)}, f32[6,512,128]{2,1,0:T(8,128)S(1)}...) custom-call(s32[2,4]{1,0:T(2,128)S(1)} %bitcast.3, s32[2,4]{1,0:T(2,128)S(1)} %bitcast.6, ...), custom_call_target="tpu_custom_call" | custom-call | tf_op jit(solution)/shard_map/pallas_call | solution.py:316
  13.9 8.7 %collective-permute-done.came = f32[136,512]{1,0:T(8,128)S(1)} collective-permute-done((f32[136,512]{1,0:T(8,128)S(1)}, f32[136,512]{1,0:T(8,128)S(1)}, u32[]{:S(2)}, u32[]{:S(2)}) %collective-permute-start) | collective-permute-done | bytes 278560 | tf_op jit(solution)/shard_map/ppermute | solution.py:16
  22.6 1.2 %shard_map.140 = (f32[512,512]{1,0:T(8,128)S(1)}, f32[328,512]{1,0:T(8,128)S(1)}, f32[256,512]{1,0:T(8,128)S(1)}, f32[128,512]{1,0:T(8,128)S(1)}) custom-call(f32[136,512]{1,0:T(8,128)S(1)} %collective-permute-done.came, bf16[768,384]{1,0:T(8,128)(2,1)S(1)} %get-tuple-element.47.first_t, f32[6,128,512]{2,1,0:T(8,128)S(1)} %get-tuple-element.48.held, ...), custom_call_target="tpu_custom_call" | custom-call | tf_op jit(solution)/shard_map/pallas_call | solution.py:316
  23.8 2.9 %collective-permute-start.3 = (f32[128,512]{1,0:T(8,128)S(1)}, f32[128,512]{1,0:T(8,128)S(1)}, u32[]{:S(2)}, u32[]{:S(2)}) collective-permute-start(f32[128,512]{1,0:T(8,128)S(1)} %get-tuple-element.54), channel_id=1, source_target_pairs={{2,1},{4,3},{6,5},{8,7},{10,9},{12,11},{14,13},{16,15},{18,17},{20... | collective-permute-start | bytes 786440 | tf_op jit(solution)/shard_map/ppermute | solution.py:16
  26.6 1.3 %collective-permute-start.2 = (f32[328,512]{1,0:T(8,128)S(1)}, f32[328,512]{1,0:T(8,128)S(1)}, u32[]{:S(2)}, u32[]{:S(2)}) collective-permute-start(f32[328,512]{1,0:T(8,128)S(1)} %get-tuple-element.53.refs_13_), channel_id=1, source_target_pairs={{2,1},{4,3},{6,5},{8,7},{10,9},{12,11},{14,13},{16,15},{18,17},{20... | collective-permute-start | bytes 2015240 | tf_op jit(solution)/shard_map/ppermute | solution.py:16
  28.0 2.5 %collective-permute-done.3.came = f32[128,512]{1,0:T(8,128)S(1)} collective-permute-done((f32[128,512]{1,0:T(8,128)S(1)}, f32[128,512]{1,0:T(8,128)S(1)}, u32[]{:S(2)}, u32[]{:S(2)}) %collective-permute-start.3) | collective-permute-done | bytes 262176 | tf_op jit(solution)/shard_map/ppermute | solution.py:16
  30.5 1.9 %collective-permute-start.4 = (f32[320,512]{1,0:T(8,128)S(1)}, f32[320,512]{1,0:T(8,128)S(1)}, u32[]{:S(2)}, u32[]{:S(2)}) collective-permute-start(f32[320,512]{1,0:T(8,128)S(1)} %get-tuple-element.63), channel_id=1, source_target_pairs={{0,1},{1,0},{2,3},{3,2},{4,5},{5,4},{6,7},{7,6},{8,9},{9,8},{10,11... | collective-permute-start | bytes 1966088 | tf_op jit(solution)/shard_map/ppermute | solution.py:16
  32.4 0.3 collective-permute-done.5.came
  32.7 1.5 %shard_map.143.base = f32[512,512]{1,0:T(8,128)S(1)} custom-call(f32[512,512]{1,0:T(8,128)S(1)} %get-tuple-element.52.smoothed, f32[512,512]{1,0:T(8,128)S(1)} %get-tuple-element.66.fix_first, f32[512,512]{1,0:T(8,128)S(1)} %get-tuple-element.67.fix_second, f32[6,512,128]{2,1,0:T(8,128)S(1)} %get-tuple-element.64.wide_first.wide, ...), custom_call_target="tpu_custom_call" | custom-call | flops 3019898880 | bytes 60 | tf_op jit(solution)/shard_map/pallas_call | solution.py:316
  34.3 0.2 collective-permute-done.4.came
  34.5 1.8 %shard_map.144 = (f32[512,512]{1,0:T(8,128)}, f32[512,512]{1,0:T(8,128)S(1)}) custom-call(f32[320,512]{1,0:T(8,128)S(1)} %collective-permute-done.4.came, f32[256,512]{1,0:T(8,128)S(1)} %get-tuple-element.60.full_first.full, f32[6,512,128]{2,1,0:T(8,128)S(1)} %get-tuple-element.64.wide_first.wide, f32[512,256]{1,0:T(8,128)S(1)} %get-tuple-element.65.column, ...), custom_call_target="tpu_custom_call" | custom-call | tf_op jit(solution)/shard_map/pallas_call | solution.py:316
  36.4 1.3 %collective-permute-done.2.came = f32[328,512]{1,0:T(8,128)S(1)} collective-permute-done((f32[328,512]{1,0:T(8,128)S(1)}, f32[328,512]{1,0:T(8,128)S(1)}, u32[]{:S(2)}, u32[]{:S(2)}) %collective-permute-start.2) | collective-permute-done | bytes 671776 | tf_op jit(solution)/shard_map/ppermute | solution.py:16
  (4 shorter events, 0.1 us)
Async XLA Ops:
  0.0 7.3 %copy-start.1 = (f32[512,512]{1,0:T(8,128)S(1)}, f32[512,512]{1,0:T(8,128)}, u32[]{:S(2)}) copy-start(f32[512,512]{1,0:T(8,128)} %source.3) | copy-start | bytes 3145732
  0.0 7.3 %copy-start.2 = (f32[4,128,128]{2,1,0:T(8,128)S(1)}, f32[4,128,128]{2,1,0:T(8,128)}, u32[]{:S(2)}) copy-start(f32[4,128,128]{2,1,0:T(8,128)} %smoother.3) | copy-start | bytes 786436
  0.0 7.3 %copy-start = (f32[4,128,128]{2,1,0:T(8,128)S(1)}, f32[4,128,128]{2,1,0:T(8,128)}, u32[]{:S(2)}) copy-start(f32[4,128,128]{2,1,0:T(8,128)} %couplings.5) | copy-start | bytes 786436
  0.0 7.3 %copy-start.7 = (s32[4,2]{0,1:T(2,128)S(1)}, s32[4,2]{0,1:T(2,128)}, u32[]{:S(2)}) copy-start(s32[4,2]{0,1:T(2,128)} %param.19) | copy-start | bytes 100
  0.0 7.3 %copy-start.8 = (s32[4,2]{0,1:T(2,128)S(1)}, s32[4,2]{0,1:T(2,128)}, u32[]{:S(2)}) copy-start(s32[4,2]{0,1:T(2,128)} %param.21) | copy-start | bytes 100
  1.8 20.8 %collective-permute-start = (f32[136,512]{1,0:T(8,128)S(1)}, f32[136,512]{1,0:T(8,128)S(1)}, u32[]{:S(2)}, u32[]{:S(2)}) collective-permute-start(f32[136,512]{1,0:T(8,128)S(1)} %get-tuple-element.38), channel_id=1, source_target_pairs={{1,2},{3,4},{5,6},{7,8},{9,10},{11,12},{13,14},{15,16},{17,18},{19... | collective-permute-start | bytes 835592 | tf_op jit(solution)/shard_map/ppermute | solution.py:16
  3.1 6.1 %collective-permute-start.1 = (f32[128,512]{1,0:T(8,128)S(1)}, f32[128,512]{1,0:T(8,128)S(1)}, u32[]{:S(2)}, u32[]{:S(2)}) collective-permute-start(f32[128,512]{1,0:T(8,128)S(1)} %get-tuple-element.43), channel_id=1, source_target_pairs={{0,1},{1,0},{2,3},{3,2},{4,5},{5,4},{6,7},{7,6},{8,9},{9,8},{10,11... | collective-permute-start | bytes 786440 | tf_op jit(solution)/shard_map/ppermute | solution.py:16
  9.1 1.5 %copy-start.3 = (f32[3,128,128]{2,1,0:T(8,128)S(1)}, f32[3,128,128]{2,1,0:T(8,128)}, u32[]{:S(2)}) copy-start(f32[3,128,128]{2,1,0:T(8,128)} %refs_3_.3) | copy-start | bytes 589828
  9.2 1.5 %copy-start.4 = (f32[1,128,128]{2,1,0:T(8,128)S(1)}, f32[1,128,128]{2,1,0:T(8,128)}, u32[]{:S(2)}) copy-start(f32[1,128,128]{2,1,0:T(8,128)} %refs_2_.3) | copy-start | bytes 196612
  9.2 1.5 %copy-start.5 = (f32[128,128]{1,0:T(8,128)S(1)}, f32[128,128]{1,0:T(8,128)}, u32[]{:S(2)}) copy-start(f32[128,128]{1,0:T(8,128)} %refs_6_.3) | copy-start | bytes 196612
  9.2 1.5 %copy-start.6 = (f32[128,128]{1,0:T(8,128)S(1)}, f32[128,128]{1,0:T(8,128)}, u32[]{:S(2)}) copy-start(f32[128,128]{1,0:T(8,128)} %refs_7_.3) | copy-start | bytes 196612
  9.2 1.5 %copy-start.9 = (s32[384]{0:T(512)S(1)}, s32[384]{0:T(512)}, u32[]{:S(2)}) copy-start(s32[384]{0:T(512)} %refs_5_.3) | copy-start | bytes 4612
  9.2 1.5 %copy-start.10 = (s32[128]{0:T(128)S(1)}, s32[128]{0:T(128)}, u32[]{:S(2)}) copy-start(s32[128]{0:T(128)} %refs_4_.3) | copy-start | bytes 1540
  9.3 23.5 %collective-permute-start.5 = (f32[320,512]{1,0:T(8,128)S(1)}, f32[320,512]{1,0:T(8,128)S(1)}, u32[]{:S(2)}, u32[]{:S(2)}) collective-permute-start(f32[320,512]{1,0:T(8,128)S(1)} %shard_map.138.refs_13_), channel_id=1, source_target_pairs={{1,2},{3,4},{5,6},{7,8},{9,10},{11,12},{13,14},{15,16},{17,18},{19... | collective-permute-start | bytes 1966088 | tf_op jit(solution)/shard_map/ppermute | solution.py:16
  23.8 6.7 %collective-permute-start.3 = (f32[128,512]{1,0:T(8,128)S(1)}, f32[128,512]{1,0:T(8,128)S(1)}, u32[]{:S(2)}, u32[]{:S(2)}) collective-permute-start(f32[128,512]{1,0:T(8,128)S(1)} %get-tuple-element.54), channel_id=1, source_target_pairs={{2,1},{4,3},{6,5},{8,7},{10,9},{12,11},{14,13},{16,15},{18,17},{20... | collective-permute-start | bytes 786440 | tf_op jit(solution)/shard_map/ppermute | solution.py:16
  26.6 11.1 %collective-permute-start.2 = (f32[328,512]{1,0:T(8,128)S(1)}, f32[328,512]{1,0:T(8,128)S(1)}, u32[]{:S(2)}, u32[]{:S(2)}) collective-permute-start(f32[328,512]{1,0:T(8,128)S(1)} %get-tuple-element.53.refs_13_), channel_id=1, source_target_pairs={{2,1},{4,3},{6,5},{8,7},{10,9},{12,11},{14,13},{16,15},{18,17},{20... | collective-permute-start | bytes 2015240 | tf_op jit(solution)/shard_map/ppermute | solution.py:16
  30.5 4.0 %collective-permute-start.4 = (f32[320,512]{1,0:T(8,128)S(1)}, f32[320,512]{1,0:T(8,128)S(1)}, u32[]{:S(2)}, u32[]{:S(2)}) collective-permute-start(f32[320,512]{1,0:T(8,128)S(1)} %get-tuple-element.63), channel_id=1, source_target_pairs={{0,1},{1,0},{2,3},{3,2},{4,5},{5,4},{6,7},{7,6},{8,9},{9,8},{10,11... | collective-permute-start | bytes 1966088 | tf_op jit(solution)/shard_map/ppermute | solution.py:16
